TPU v7x, 32 devices: a whole 2x2x4 slice. The times are simulated.
32 devices in a mesh: req: 16 (over z, y, core), tp: 2 (over x).
Axes of the slice: x: 2, y: 2, z: 4, core: 2. Of those that a mesh axis runs over, the one named last changes fastest.
Arguments:
- states: bfloat16 [4096, 3072], P('req', 'tp'), may hold values from -12 to 12
- query_weight: bfloat16 [3072, 1536], P(None, 'tp'), may hold values from -0.75 to 0.75
- key_value_weight: bfloat16 [3072, 512], P(None, 'tp'), may hold values from -0.75 to 0.75
- lengths: int32 [16], P('req'), may hold values from 1 to 256, 2048 in all
- adapter_ids: int32 [16], P('req'), may hold values from 0 to 63, as said below
- adapter_slot: int32 [64], replicated, may hold values from 0 to 63, as said below
- down_store: bfloat16 [64, 3072, 32], P('req', 'tp'), may hold values from -0.109375 to 0.109375
- query_up_store: bfloat16 [64, 16, 1536], P('req', None, 'tp'), may hold values from -1.5 to 1.5
- key_value_store: bfloat16 [64, 16, 512], P('req', None, 'tp'), may hold values from -1.5 to 1.5
Outputs:
- context: bfloat16 [4096, 1536], P('req', 'tp')
Inputs may be any that keep to these rules, and one draw needn't show every extreme that they name: `adapter_ids`: exactly 16 distinct adapters are named among all 16 requests. `adapter_slot`: distinct adapters have distinct rows.
All inputs are finite; a program needn't handle non-finite values. No bound on the sum of `lengths` on one device may be relied on, other than what follows from the above.
Results may differ from a plain program's by a relative error of at most 0.0072.
Values may be sent and summed in bfloat16 or wider, within the bound.
A program may use at most 64 MiB of HBM per device.

v0:
```python
import math

import jax
import jax.numpy as jnp
from jax import lax
from jax.sharding import PartitionSpec as P

HEADS = 12
HEAD_DIM = 128


adapter_scale = 0.5
rope_base = 100000000000.0


def rotate(field):
    half = field.shape[-1] // 2
    count = field.shape[-3]
    position = jnp.arange(count).astype(jnp.float32)
    inverse = rope_base ** (-(jnp.arange(half).astype(jnp.float32) * 2.0) / field.shape[-1])
    angle = position[:, None] * inverse[None, :]
    cosine = jnp.cos(angle)[:, None, :]
    sine = jnp.sin(angle)[:, None, :]
    first_half = field[..., :half]
    second_half = field[..., half:]
    return jnp.concatenate(
        [first_half * cosine - second_half * sine, second_half * cosine + first_half * sine],
        axis=-1,
    )


def lookup_slots(wanted, adapter_slot):
    table = jnp.arange(adapter_slot.shape[0], dtype=jnp.int32)
    matches = wanted[:, None] == table[None, :]
    return jnp.sum(jnp.where(matches, adapter_slot[None, :], 0), axis=1)


def local(
    states,
    query_weight,
    key_value_weight,
    lengths,
    adapter_ids,
    adapter_slot,
    down_store,
    query_up_store,
    key_value_store,
):
    tp_index = lax.axis_index("tp")
    req_dev = lengths.shape[0]
    rows_total = states.shape[0]
    slot_len = rows_total // req_dev
    q_cols = query_weight.shape[1]
    kv_cols = key_value_weight.shape[1]
    heads_here = q_cols // HEAD_DIM
    pooled = (
        lax.all_gather(down_store, "req", axis=0, tiled=True),
        lax.all_gather(query_up_store, "req", axis=0, tiled=True),
        lax.all_gather(key_value_store, "req", axis=0, tiled=True),
    )
    own_slots = lookup_slots(adapter_ids, adapter_slot)
    adapter_down, adapter_query, adapter_pair = (
        jnp.take(member, own_slots, axis=0) for member in pooled
    )
    full_down = lax.all_gather(adapter_down, "tp", axis=1, tiled=True)
    piece = lax.all_gather(states, "tp", axis=1, tiled=True)
    width = piece.shape[1]
    grouped = piece.reshape(req_dev, slot_len, width)
    query_total = jnp.dot(piece, query_weight, preferred_element_type=jnp.float32)
    key_value_sum = jnp.dot(piece, key_value_weight, preferred_element_type=jnp.float32)
    rank_sum = jnp.einsum("rsd,rdk->rsk", grouped, full_down, preferred_element_type=jnp.float32)
    rank_mid = rank_sum.astype(jnp.bfloat16)
    rank_cols = rank_mid.shape[2] // 2
    query_addition = jnp.einsum(
        "rsk,rkc->rsc",
        rank_mid[:, :, :rank_cols],
        adapter_query,
        preferred_element_type=jnp.float32,
    ).reshape(rows_total, q_cols)
    key_value_extra = jnp.einsum(
        "rsk,rkc->rsc", rank_mid[:, :, rank_cols:], adapter_pair, preferred_element_type=jnp.float32
    ).reshape(rows_total, kv_cols)
    query_plain = query_total + adapter_scale * query_addition
    key_value_own = (key_value_sum + adapter_scale * key_value_extra).astype(jnp.bfloat16)
    pair_all = lax.all_gather(key_value_own, "tp", axis=1, tiled=True)
    key_width = pair_all.shape[1] // 2
    kv_heads = key_width // HEAD_DIM
    group = HEADS // kv_heads
    kv_index = tp_index * heads_here // group
    key_block = lax.dynamic_slice_in_dim(pair_all, kv_index * HEAD_DIM, HEAD_DIM, 1)
    value_block = lax.dynamic_slice_in_dim(pair_all, key_width + kv_index * HEAD_DIM, HEAD_DIM, 1)
    queries = rotate(query_plain.reshape(req_dev, slot_len, heads_here, HEAD_DIM)).astype(
        jnp.bfloat16
    )
    keys_one = rotate(key_block.astype(jnp.float32).reshape(req_dev, slot_len, 1, HEAD_DIM)).astype(
        jnp.bfloat16
    )[:, :, 0, :]
    values_one = value_block.reshape(req_dev, slot_len, HEAD_DIM)
    scale = 1.0 / math.sqrt(HEAD_DIM)
    scores = (
        jnp.einsum("rqhd,rkd->rhqk", queries, keys_one, preferred_element_type=jnp.float32) * scale
    )
    position = jnp.arange(slot_len, dtype=jnp.int32)
    allowed = (position[None, None, :] <= position[None, :, None]) & (
        position[None, None, :] < lengths[:, None, None]
    )
    scores = jnp.where(allowed[:, None, :, :], scores, -jnp.inf)
    highest = jnp.max(scores, axis=-1, keepdims=True)
    expo = jnp.exp(scores - highest)
    weights = (expo / jnp.sum(expo, axis=-1, keepdims=True)).astype(jnp.bfloat16)
    context = jnp.einsum("rhqk,rkd->rqhd", weights, values_one, preferred_element_type=jnp.float32)
    live_rows = position[None, :] < lengths[:, None]
    context = jnp.where(live_rows[:, :, None, None], context, 0.0)
    return context.reshape(rows_total, q_cols).astype(jnp.bfloat16)


def solution(mesh):
    return jax.shard_map(
        local,
        mesh=mesh,
        in_specs=(
            P("req", "tp"),
            P(None, "tp"),
            P(None, "tp"),
            P("req"),
            P("req"),
            P(),
            P("req", "tp", None),
            P("req", None, "tp"),
            P("req", None, "tp"),
        ),
        out_specs=P("req", "tp"),
        check_vma=False,
    )
```

profile of v0, /device:TPU:0, one launch (start us, length us, event | category | flops | bytes accessed | tf_op | source)
XLA Modules:
  0.0 164.6 jit_solution(17545245122745066487)
XLA Ops:
  6.5 0.0 copy-start
  6.5 0.0 copy-start.3
  6.5 0.0 all-gather.4.cloned.1.call-start
  6.5 0.7 all-gather.4.cloned.1.call-update
  7.3 0.0 all-gather.6.cloned.1.call-start
  7.3 0.7 all-gather.6.cloned.1.call-update
  8.0 0.0 all-gather.8.cloned.1.call-start
  8.1 0.7 all-gather.8.cloned.1.call-update
  9.4 1.3 fusion.38
  13.3 0.0 copy-start.5
  13.4 0.0 copy-start.6
  13.4 0.0 copy-start.4
  13.4 0.7 fusion.13
  14.1 0.0 copy-done.4
  14.1 1.2 multiply_cosine_fusion
  15.4 0.0 copy-done.5
  15.4 0.0 copy-done.6
  15.4 0.0 copy-done.3
  15.4 26.1 %all_gather.21 = bf16[64,16,256]{2,1,0:T(8,128)(2,1)} all-gather(bf16[4,16,256]{2,1,0:T(8,128)(2,1)S(1)} %copy-done.3), channel_id=1, replica_groups=mesh['req'=16,'tp'=2] {'req'}, dimensions={0}, use_global_device_ids=true | all-gather | bytes 557056 | tf_op jit(solution)/shard_map/all_gather | solution.py:59
  41.4 0.0 all-gather.4.cloned.1.call-done
  41.4 0.0 copy-done
  41.4 0.0 copy-start.1
  41.4 2.8 %fusion.44 = f32[256,256]{1,0:T(8,128)} fusion(bf16[256,3072]{1,0:T(8,128)(2,1)} %all-gather.4.cloned.1.call-done, bf16[3072,256]{1,0:T(8,128)(2,1)S(1)} %copy-done), kind=kOutput, calls=%fused_computation.69 | convolution fusion | flops 402653184 | bytes 3407872 | tf_op jit(solution)/shard_map/dot_general | solution.py:70
  44.2 0.0 copy-done.1
  44.2 4.7 %fusion.45 = f32[256,768]{1,0:T(8,128)} fusion(bf16[256,3072]{1,0:T(8,128)(2,1)S(1)} %copy-done.1, bf16[3072,768]{1,0:T(8,128)(2,1)} %param.10), kind=kOutput, calls=%fused_computation.70 | convolution fusion | flops 1207959552 | bytes 7077888 | tf_op jit(solution)/shard_map/dot_general | solution.py:69
  48.9 54.1 %all-gather.6.cloned.1.call-done = bf16[64,1536,32]{1,2,0:T(8,128)(2,1)} async-done(((bf16[4,1536,32]{1,2,0:T(8,128)(2,1)}), bf16[64,1536,32]{1,2,0:T(8,128)(2,1)}) %all-gather.6.cloned.1.call-update) | async-done | bytes 6291472 | tf_op jit(solution)/shard_map/all_gather | solution.py:57
  103.0 0.9 dynamic-slice_select_fusion
  103.9 5.6 %all_gather.20 = bf16[1,3072,32]{1,2,0:T(8,128)(2,1)S(1)} all-gather(bf16[1,1536,32]{1,2,0:T(8,128)(2,1)S(1)} %dynamic-slice_select_fusion), channel_id=1, replica_groups=mesh['req'=16,'tp'=2] {'tp'}, dimensions={1}, use_global_device_ids=true | all-gather | bytes 294912 | tf_op jit(solution)/shard_map/all_gather | solution.py:65
  109.6 0.6 fusion.6
  110.1 33.5 %all-gather.8.cloned.1.call-done = bf16[64,16,768]{2,1,0:T(8,128)(2,1)} async-done(((bf16[4,16,768]{2,1,0:T(8,128)(2,1)}), bf16[64,16,768]{2,1,0:T(8,128)(2,1)}) %all-gather.8.cloned.1.call-update) | async-done | bytes 1572880 | tf_op jit(solution)/shard_map/all_gather | solution.py:58
  143.6 1.4 fusion.1
  145.1 0.3 copy.21
  145.3 0.1 fusion.42
  145.4 0.3 copy.30
  145.7 0.3 copy.31
  145.9 1.2 fusion.5
  147.1 6.3 %all_gather.22 = bf16[256,512]{1,0:T(8,128)(2,1)S(1)} all-gather(bf16[256,256]{1,0:T(8,128)(2,1)S(1)} %fusion.5), channel_id=1, replica_groups=mesh['req'=16,'tp'=2] {'tp'}, dimensions={1}, use_global_device_ids=true | all-gather | bytes 393216 | tf_op jit(solution)/shard_map/all_gather | solution.py:85
  153.5 0.0 copy-start.2
  153.5 1.3 fusion.28
  154.8 1.2 fusion.8
  156.0 0.0 copy-done.2
  156.0 0.0 copy-start.7
  156.0 0.5 fusion.43
  156.5 0.2 fusion
  156.7 0.0 copy-done.7
  156.7 0.4 fusion.3
  157.2 0.9 copy.26
  (4 shorter events, 0.0 us)
Async XLA Ops:
  6.5 34.9 %copy-start = (bf16[3072,256]{1,0:T(8,128)(2,1)S(1)}, bf16[3072,256]{1,0:T(8,128)(2,1)}, u32[]{:S(2)}) copy-start(bf16[3072,256]{1,0:T(8,128)(2,1)} %param.11) | copy-start | bytes 4718596
  6.5 8.8 %copy-start.3 = (bf16[4,16,256]{2,1,0:T(8,128)(2,1)S(1)}, bf16[4,16,256]{2,1,0:T(8,128)(2,1)}, u32[]{:S(2)}) copy-start(bf16[4,16,256]{2,1,0:T(8,128)(2,1)} %param.17) | copy-start | bytes 98308
  6.5 34.9 %all-gather.4.cloned.1.call-start = ((), (), s32[]{:S(2)}) async-start(), calls=%async_computation | async-start | bytes 2359296 | tf_op jit(solution)/shard_map/all_gather | solution.py:66
  7.3 95.8 %all-gather.6.cloned.1.call-start = ((), (), s32[]{:S(2)}) async-start(), calls=%async_computation.1 | async-start | bytes 6684672 | tf_op jit(solution)/shard_map/all_gather | solution.py:57
  8.0 135.6 %all-gather.8.cloned.1.call-start = ((), (), s32[]{:S(2)}) async-start(), calls=%async_computation.2 | async-start | bytes 1671168 | tf_op jit(solution)/shard_map/all_gather | solution.py:58
  13.3 2.0 %copy-start.5 = (f32[64]{0:T(128)}, f32[64]{0:T(128)S(1)}, u32[]{:S(2)}) copy-start(f32[64]{0:T(128)S(1)} %multiply_power_fusion) | copy-start | bytes 772
  13.4 2.0 %copy-start.6 = (pred[256]{0:T(512)(128)(4,1)}, pred[256]{0:T(512)(128)(4,1)S(1)}, u32[]{:S(2)}) copy-start(pred[256]{0:T(512)(128)(4,1)S(1)} %iota_compare_fusion.1) | copy-start | bytes 772
  13.4 0.7 copy-start.4
  41.4 2.8 %copy-start.1 = (bf16[256,3072]{1,0:T(8,128)(2,1)S(1)}, bf16[256,3072]{1,0:T(8,128)(2,1)}, u32[]{:S(2)}) copy-start(bf16[256,3072]{1,0:T(8,128)(2,1)} %all-gather.4.cloned.1.call-done) | copy-start | bytes 4718596
  153.5 2.5 %copy-start.2 = (pred[256,256]{0,1:T(8,128)(4,1)S(1)}, pred[256,256]{0,1:T(8,128)(4,1)}, u32[]{:S(2)}) copy-start(pred[256,256]{0,1:T(8,128)(4,1)} %fusion.13) | copy-start | bytes 196612
  156.0 0.8 copy-start.7
Sparse Core Ops, SparseCore 0:
  8.9 29.8 all-gather.3
  41.1 61.8 all-gather.5
  105.3 38.2 all-gather.7
where the time goes:
time: 165 us
  waiting for transfers between devices  89.7 us (54%)
  blocking collectives  38 us (23%)
  between operations  16.5 us (10%)
  matrix products  11.7 us (7%)
  other arithmetic  6.92 us (4%)
  local copies, waits for them, and re-layouts  1.8 us (1%)
    all_gather x1, waiting for transfers between devices, local(): lax.all_gather(down_store, 'req', axis=0, tiled=True)  54.1 us
    all_gather x1, waiting for transfers between devices, local(): lax.all_gather(query_up_store, 'req', axis=0, tiled=True)  33.5 us
    all_gather x1, blocking collectives, local(): lax.all_gather(key_value_store, 'req', axis=0, tiled=True)  26.1 us
    all_gather x1, blocking collectives, local(): pair_all = lax.all_gather(key_value_own, 'tp', axis=1, tiled=True)  6.34 us
    all_gather x1, blocking collectives, local(): full_down = lax.all_gather(adapter_down, 'tp', axis=1, tiled=True)  5.64 us
    dot_general x1, matrix products, local(): jnp.dot(piece, query_weight, preferred_element_type=jnp.float32)  4.7 us
  transfers between devices with their start and end apart: 3, of which 2 were waited for; matrix products, arithmetic and copies ran while one was open for 7% of the time, Pallas kernels for 0%

commit v1 on v0

--- a/solution.py
+++ b/solution.py
@@ -1,8 +1,12 @@
+import functools
 import math
 
 import jax
 import jax.numpy as jnp
+import numpy as np
 from jax import lax
+from jax.experimental import pallas as pl
+from jax.experimental.pallas import tpu as pltpu
 from jax.sharding import PartitionSpec as P
 
 HEADS = 12
@@ -114,9 +118,389 @@
     return context.reshape(rows_total, q_cols).astype(jnp.bfloat16)
 
 
+MESH = pl.DeviceIdType.MESH
+PIECES = 4
+GROUPS = ((0, 192), (192, 64))
+
+
+def fused(
+    planes,
+    ids,
+    slots,
+    lengths,
+    states,
+    wq,
+    wkv,
+    rows,
+    cosine,
+    sine,
+    out,
+    own_st,
+    other_st,
+    w_own,
+    w_other,
+    total,
+    plane,
+    ids_own,
+    ids_in,
+    leaving,
+    landed,
+    down,
+    ups,
+    mid_out,
+    mid_in,
+    kv_own,
+    kv_in,
+    local_sem,
+    st_send,
+    st_recv,
+    y_send,
+    y_recv,
+    c_send,
+    c_recv,
+    f_send,
+    f_recv,
+    i_send,
+    i_recv,
+    z_send,
+    z_recv,
+    m_send,
+    m_recv,
+    kv_send,
+    kv_recv,
+):
+    r = lax.axis_index("req")
+    tp = lax.axis_index("tp")
+    per_plane = 4
+    count = planes * per_plane
+    half = own_st.shape[1]
+    q_cols = wq.shape[1]
+    tokens = own_st.shape[0]
+    step = tokens // PIECES
+    mine = rows.shape[1]
+    core_peer = r + 1 - 2 * (r % 2)
+    y_peer = r + 2 - 4 * ((r // 2) % 2)
+    z_peers = [(r + per_plane * d) % count for d in range(1, planes)]
+    across = 1 - tp
+    base = (r // per_plane) * (per_plane * mine)
+
+    def place(index):
+        return pl.ds((index % per_plane) * mine, mine)
+
+    def remote(src, dst, send, recv, who):
+        return pltpu.make_async_remote_copy(
+            src_ref=src, dst_ref=dst, send_sem=send, recv_sem=recv, device_id=who, device_id_type=MESH
+        )
+
+    own_rows = pl.ds(pl.multiple_of(tp * half, half), half)
+    other_rows = pl.ds(pl.multiple_of(across * half, half), half)
+    loads = [
+        pltpu.make_async_copy(states, own_st, local_sem.at[0]),
+        pltpu.make_async_copy(wq.at[own_rows], w_own.at[:, :q_cols], local_sem.at[1]),
+        pltpu.make_async_copy(wkv.at[own_rows], w_own.at[:, q_cols:], local_sem.at[2]),
+        pltpu.make_async_copy(wq.at[other_rows], w_other.at[:, :q_cols], local_sem.at[3]),
+        pltpu.make_async_copy(wkv.at[other_rows], w_other.at[:, q_cols:], local_sem.at[4]),
+        pltpu.make_async_copy(rows, plane.at[:, place(r)], local_sem.at[5]),
+    ]
+    for copy in loads:
+        copy.start()
+
+    ids_own[...] = jnp.full(ids_own.shape, slots[ids[0]], jnp.int32)
+
+    barrier = pltpu.get_barrier_semaphore()
+    for peer in [core_peer, y_peer] + z_peers:
+        pl.semaphore_signal(barrier, inc=1, device_id={"req": peer}, device_id_type=MESH)
+    pl.semaphore_signal(barrier, inc=1, device_id={"tp": across}, device_id_type=MESH)
+    pl.semaphore_wait(barrier, planes + 2)
+
+    id_copies = [
+        remote(ids_own, ids_in.at[d], i_send.at[d], i_recv.at[d], {"req": peer})
+        for d, peer in enumerate(z_peers)
+    ]
+    st_copies = [
+        remote(
+            states.at[pl.ds(p * step, step)],
+            other_st.at[pl.ds(p * step, step)],
+            st_send.at[p],
+            st_recv.at[p],
+            {"tp": across},
+        )
+        for p in range(PIECES)
+    ]
+    y_copies = [
+        remote(rows.at[k], plane.at[k, place(r)], y_send.at[k], y_recv.at[k], {"req": y_peer})
+        for k in range(4)
+    ]
+    c_copies = [
+        remote(rows.at[k], plane.at[k, place(r)], c_send.at[k], c_recv.at[k], {"req": core_peer})
+        for k in range(4)
+    ]
+    f_copies = [
+        remote(
+            plane.at[k, place(y_peer)],
+            plane.at[k, place(y_peer)],
+            f_send.at[k],
+            f_recv.at[k],
+            {"req": core_peer},
+        )
+        for k in range(4)
+    ]
+    for copy in id_copies:
+        copy.start()
+    for k in range(4):
+        st_copies[k].start()
+        y_copies[k].start()
+        c_copies[k].start()
+
+    for n in (0, 1, 2):
+        loads[n].wait()
+    total[...] = jnp.dot(own_st[...], w_own[...], preferred_element_type=jnp.float32)
+    loads[5].wait()
+    for copy in id_copies:
+        copy.wait_recv()
+    loads[3].wait()
+    loads[4].wait()
+
+    def add_piece(p):
+        st_copies[p].wait_recv()
+        span = pl.ds(p * step, step)
+        total[span] += jnp.dot(other_st[span], w_other[...], preferred_element_type=jnp.float32)
+
+    z_copies = []
+    selves = []
+    for k in range(4):
+        y_copies[k].wait_recv()
+        f_copies[k].start()
+        c_copies[k].wait_recv()
+        f_copies[k].wait_recv()
+
+        def pick(j, sums, k=k):
+            record = plane[k, j]
+            made = []
+            for d in range(planes):
+                wanted = ids_own[...] if d == 0 else ids_in[planes - 1 - d]
+                flag = jnp.where(wanted == base + j, 1.0, 0.0).astype(jnp.bfloat16)
+                flag = jnp.concatenate([flag] * (record.shape[1] // flag.shape[1]), axis=1)
+                made.append(sums[d] + flag * record)
+            return tuple(made)
+
+        zero = jnp.zeros(plane.shape[2:], jnp.bfloat16)
+        sums = lax.fori_loop(0, per_plane * mine, pick, (zero,) * planes)
+        for d in range(1, planes):
+            leaving[k, d - 1] = sums[d]
+        ups[k] = sums[0]
+        sent = [
+            remote(
+                leaving.at[k, d],
+                landed.at[k, d],
+                z_send.at[k, d],
+                z_recv.at[k, d],
+                {"req": peer},
+            )
+            for d, peer in enumerate(z_peers)
+        ]
+        for copy in sent:
+            copy.start()
+        z_copies.append(sent)
+        if k in (1, 3):
+            add_piece(k // 2)
+
+    def take(k):
+        for copy in z_copies[k]:
+            copy.wait_recv()
+        record = ups[k]
+        for d in range(planes - 1):
+            record = record + landed[k, d]
+        return record
+
+    rank = down.shape[0] // 2
+    wide = plane.shape[3]
+    left = half - wide
+    down[0:rank, 0:wide] = take(0)
+    down[rank:, 0:wide] = take(1)
+    tail = take(2)
+    down[0:rank, wide:] = tail[:, :left]
+    down[rank:, wide:] = tail[:, left:]
+    mid_out[...] = lax.dot_general(
+        down[...], own_st[...], (((1,), (1,)), ((), ())), preferred_element_type=jnp.float32
+    )
+    mid_copy = remote(mid_out, mid_in, m_send.at[0], m_recv.at[0], {"tp": across})
+    mid_copy.start()
+    up = take(3)
+    col = lax.broadcasted_iota(jnp.int32, (rank, wide), 1)
+    empty = jnp.zeros_like(up)
+    lifted = jnp.concatenate([jnp.where(col < q_cols, up, empty), jnp.where(col < q_cols, empty, up)], axis=0)
+    add_piece(2)
+    mid_copy.wait_recv()
+    mid = jnp.transpose(mid_out[...] + mid_in[...]).astype(jnp.bfloat16)
+    extra = 0.5 * jnp.dot(mid, lifted, preferred_element_type=jnp.float32)
+    total[...] += extra
+
+    kv_copies = []
+    keep = pl.ds(pl.multiple_of(tp * HEAD_DIM, HEAD_DIM), HEAD_DIM)
+    give = pl.ds(pl.multiple_of(across * HEAD_DIM, HEAD_DIM), HEAD_DIM)
+    for g, (first, size) in enumerate(GROUPS):
+        if g == 1:
+            add_piece(3)
+        span = pl.ds(first, size)
+        kv_own[span] = total[span, q_cols:].astype(jnp.bfloat16)
+        copy = remote(
+            kv_own.at[span, give], kv_in.at[span], kv_send.at[g], kv_recv.at[g], {"tp": across}
+        )
+        copy.start()
+        kv_copies.append(copy)
+
+    scale = 1.0 / math.sqrt(HEAD_DIM)
+    length = lengths[0]
+
+    def turn(x, span):
+        return (x * cosine[span] + pltpu.roll(x, HEAD_DIM // 2, 1) * sine[span]).astype(jnp.bfloat16)
+
+    key_parts = []
+    value_parts = []
+    for g, (first, size) in enumerate(GROUPS):
+        span = pl.ds(first, size)
+        turned = [
+            turn(total[span, h * HEAD_DIM : (h + 1) * HEAD_DIM], span)
+            for h in range(q_cols // HEAD_DIM)
+        ]
+        kv_copies[g].wait_recv()
+        kept = kv_own[span, keep]
+        came = kv_in[span]
+        first_side = jnp.full(kept.shape, tp, jnp.int32) == 0
+        key = jnp.where(first_side, kept.astype(jnp.float32), came.astype(jnp.float32))
+        value = jnp.where(first_side, came.astype(jnp.float32), kept.astype(jnp.float32))
+        key_parts.append(turn(key, span))
+        value_parts.append(value.astype(jnp.bfloat16))
+        reach = first + size
+        keys = jnp.concatenate(key_parts, axis=0) if g else key_parts[0]
+        values = jnp.concatenate(value_parts, axis=0) if g else value_parts[0]
+        row = lax.broadcasted_iota(jnp.int32, (size, reach), 0) + first
+        column = lax.broadcasted_iota(jnp.int32, (size, reach), 1)
+        allowed = (column <= row) & (column < length)
+        live = lax.broadcasted_iota(jnp.int32, (size, HEAD_DIM), 0) + first < length
+        for h, query in enumerate(turned):
+            scores = lax.dot_general(
+                query, keys, (((1,), (1,)), ((), ())), preferred_element_type=jnp.float32
+            )
+            scores = jnp.where(allowed, scores * scale, -jnp.inf)
+            expo = jnp.exp(scores - jnp.max(scores, axis=1, keepdims=True))
+            weights = (expo / jnp.sum(expo, axis=1, keepdims=True)).astype(jnp.bfloat16)
+            mixed = jnp.dot(weights, values, preferred_element_type=jnp.float32)
+            out[span, h * HEAD_DIM : (h + 1) * HEAD_DIM] = jnp.where(live, mixed, 0.0).astype(
+                jnp.bfloat16
+            )
+
+    for copy in id_copies + st_copies + y_copies + c_copies + f_copies + [mid_copy] + kv_copies:
+        copy.wait_send()
+    for sent in z_copies:
+        for copy in sent:
+            copy.wait_send()
+
+
+def tables(tokens):
+    half = HEAD_DIM // 2
+    position = np.arange(tokens, dtype=np.float32)
+    inverse = np.float32(rope_base) ** (-(np.arange(half, dtype=np.float32) * 2.0) / HEAD_DIM).astype(
+        np.float32
+    )
+    angle = position[:, None] * inverse[None, :].astype(np.float32)
+    cosine = np.cos(angle)
+    sine = np.sin(angle)
+    return (
+        np.concatenate([cosine, cosine], axis=1).astype(np.float32),
+        np.concatenate([-sine, sine], axis=1).astype(np.float32),
+    )
+
+
+def local_fused(
+    planes,
+    states,
+    query_weight,
+    key_value_weight,
+    lengths,
+    adapter_ids,
+    adapter_slot,
+    down_store,
+    query_up_store,
+    key_value_store,
+):
+    tokens, half = states.shape
+    q_cols = query_weight.shape[1]
+    kv_cols = key_value_weight.shape[1]
+    cols = q_cols + kv_cols
+    mine, rank = query_up_store.shape[:2]
+    turned = jnp.transpose(down_store, (0, 2, 1))
+    rows = jnp.stack(
+        [
+            turned[:, :rank, :cols],
+            turned[:, rank:, :cols],
+            jnp.concatenate([turned[:, :rank, cols:], turned[:, rank:, cols:]], axis=2),
+            jnp.concatenate([query_up_store, key_value_store], axis=2),
+        ]
+    )
+    cosine, sine = tables(tokens)
+    peers = planes - 1
+    vmem = pl.BlockSpec(memory_space=pltpu.VMEM)
+    smem = pl.BlockSpec(memory_space=pltpu.SMEM)
+    hbm = pl.BlockSpec(memory_space=pl.ANY)
+    bf16, f32 = jnp.bfloat16, jnp.float32
+    dma = pltpu.SemaphoreType.DMA
+    return pl.pallas_call(
+        functools.partial(fused, planes),
+        out_shape=jax.ShapeDtypeStruct((tokens, q_cols), bf16),
+        in_specs=[smem, smem, smem, hbm, hbm, hbm, hbm, vmem, vmem],
+        out_specs=vmem,
+        scratch_shapes=[
+            pltpu.VMEM((tokens, half), bf16),
+            pltpu.VMEM((tokens, half), bf16),
+            pltpu.VMEM((half, cols), bf16),
+            pltpu.VMEM((half, cols), bf16),
+            pltpu.VMEM((tokens, cols), f32),
+            pltpu.VMEM((4, 4 * mine, rank, cols), bf16),
+            pltpu.VMEM((16, 128), jnp.int32),
+            pltpu.VMEM((peers, 16, 128), jnp.int32),
+            pltpu.VMEM((4, peers, rank, cols), bf16),
+            pltpu.VMEM((4, peers, rank, cols), bf16),
+            pltpu.VMEM((2 * rank, half), bf16),
+            pltpu.VMEM((4, rank, cols), bf16),
+            pltpu.VMEM((2 * rank, tokens), f32),
+            pltpu.VMEM((2 * rank, tokens), f32),
+            pltpu.VMEM((tokens, kv_cols), bf16),
+            pltpu.VMEM((tokens, HEAD_DIM), bf16),
+            dma((6,)),
+            dma((PIECES,)),
+            dma((PIECES,)),
+            dma((4,)),
+            dma((4,)),
+            dma((4,)),
+            dma((4,)),
+            dma((4,)),
+            dma((4,)),
+            dma((peers,)),
+            dma((peers,)),
+            dma((4, peers)),
+            dma((4, peers)),
+            dma((1,)),
+            dma((1,)),
+            dma((len(GROUPS),)),
+            dma((len(GROUPS),)),
+        ],
+        compiler_params=pltpu.CompilerParams(
+            collective_id=0, has_side_effects=True, vmem_limit_bytes=40 * 1024 * 1024
+        ),
+        name="fused_attention",
+    )(adapter_ids, adapter_slot, lengths, states, query_weight, key_value_weight, rows, cosine, sine)
+
+
 def solution(mesh):
+    planes = mesh.shape["req"] // 4
+    if mesh.shape["tp"] == 2 and planes == 4:
+        body = functools.partial(local_fused, planes)
+    else:
+        body = local
     return jax.shard_map(
-        local,
+        body,
         mesh=mesh,
         in_specs=(
             P("req", "tp"),

time: 165 us -> 47 us (0.28)
  waiting for transfers between devices: 89.7 us -> 0 us
  blocking collectives: 38 us -> 0 us
  Pallas kernels: 0 us -> 34.3 us
  between operations: 16.5 us -> 1.34 us
  matrix products: 11.7 us -> 0 us
  local copies, waits for them, and re-layouts: 1.8 us -> 8.96 us
  other arithmetic: 6.92 us -> 2.01 us
    all_gather x3 -> x0, waiting for transfers between devices: 87.6 us -> none  [the longest x1 54.1 us: local(): lax.all_gather(down_store, 'req', axis=0, tiled=True)]
    all_gather x3 -> x0, blocking collectives: 38 us -> none  [the longest x1 26.1 us: local(): lax.all_gather(key_value_store, 'req', axis=0, tiled=True)]
    pallas_call x0 -> x1, Pallas kernels: none -> 34.3 us  [local_fused(): pl.pallas_call(functools.partial(fused, planes), out_shape=jax.ShapeDtype...]
    dot_general x7 -> x0, matrix products: 11.7 us -> none  [the longest x1 4.7 us: local(): jnp.dot(piece, query_weight, preferred_element_type=jnp.float32)]
    unnamed x18 -> x13, local copies, waits for them, and re-layouts: 0.56 us -> 8.08 us
    concatenate x2 -> x0, other arithmetic: 2.45 us -> none  [rotate(): jnp.concatenate([first_half * cosine - second_half * sine, second_half *...]
    unnamed x3 -> x0, waiting for transfers between devices: 2.09 us -> none
    another operation x0 -> x3, other arithmetic: none -> 2.01 us  [local_fused(): jnp.stack([turned[:, :rank, :cols], turned[:, rank:, :cols], jnp.concaten...]
  transfers between devices with their start and end apart: 3 -> 0, of which waited for: 2 -> 0; matrix products, arithmetic and copies ran while one was open for 7% -> 0% of each run, Pallas kernels for 0% -> 0%
where the time goes in v1:
time: 47 us; the launch traced here: 46.6 us
  Pallas kernels  34.3 us (73%)
  local copies, waits for them, and re-layouts  8.96 us (19%)
  other arithmetic  2.01 us (4%)
  between operations  1.34 us (3%)
    pallas_call x1, Pallas kernels, local_fused(): pl.pallas_call(functools.partial(fused, planes), out_shape=jax.ShapeDtype...  34.3 us
    unnamed x13, local copies, waits for them, and re-layouts  8.08 us
    another operation x3, other arithmetic, local_fused(): jnp.stack([turned[:, :rank, :cols], turned[:, rank:, :cols], jnp.concaten...  2.01 us

profile of v1, /device:TPU:0, one launch (start us, length us, event | category | flops | bytes accessed | tf_op | source)
XLA Modules:
  0.0 46.6 jit_solution(5063734947345963250)
XLA Ops:
  0.0 0.9 %fusion = (bf16[4,16,512]{2,1,0:T(8,128)(2,1)S(1)}, bf16[4,16,512]{2,1,0:T(8,128)(2,1)S(1)}) fusion(bf16[4,32,1536]{2,1,0:T(8,128)(2,1)} %bitcast.9), kind=kLoop, calls=%fused_computation.5 | loop fusion | bytes 262144 | tf_op jit(solution)/shard_map/slice | solution.py:438
  0.9 1.0 %slice_bitcast_fusion.1 = (bf16[1,4,16,1024]{3,2,1,0:T(8,128)(2,1)S(1)}, bf16[1,4,16,1024]{3,2,1,0:T(8,128)(2,1)S(1)}, bf16[1,4,16,1024]{3,2,1,0:T(8,128)(2,1)S(1)}) fusion(bf16[4,32,1536]{2,1,0:T(8,128)(2,1)} %bitcast.10, bf16[4,16,512]{2,1,0:T(8,128)(2,1)S(1)} %get-tuple-element.8, bf16[4,16,512]{2,1,0:T(8,128)(2,1)S(1)} %get-tuple-element.7), kind=kLoop, calls=%fused_computation.2 | loop fusion | flops 262144 | bytes 786432 | tf_op jit(solution)/shard_map/stack | solution.py:434
  1.9 0.9 %maximum_bitcast_fusion.1 = bf16[1,4,16,1024]{3,2,1,0:T(8,128)(2,1)S(1)} fusion(bf16[4,16,256]{2,1,0:T(8,128)(2,1)} %param.19, bf16[4,16,768]{2,1,0:T(8,128)(2,1)} %param.18), kind=kLoop, calls=%fused_computation.4 | loop fusion | flops 262144 | bytes 262144 | tf_op jit(solution)/shard_map/stack | solution.py:434
  2.8 0.1 pad_maximum_fusion.rows
  4.2 0.0 copy-start
  4.2 2.3 %copy-done = bf16[3072,768]{1,0:T(8,128)(2,1)S(1)} copy-done((bf16[3072,768]{1,0:T(8,128)(2,1)S(1)}, bf16[3072,768]{1,0:T(8,128)(2,1)}, u32[]{:S(2)}) %copy-start) | copy-done | bytes 4718616
  6.5 0.0 copy-start.1
  6.5 1.4 %copy-done.1 = bf16[3072,256]{1,0:T(8,128)(2,1)S(1)} copy-done((bf16[3072,256]{1,0:T(8,128)(2,1)S(1)}, bf16[3072,256]{1,0:T(8,128)(2,1)}, u32[]{:S(2)}) %copy-start.1) | copy-done | bytes 1572888
  8.0 0.0 copy-start.2
  8.0 1.1 %copy-done.2 = bf16[256,1536]{1,0:T(8,128)(2,1)S(1)} copy-done((bf16[256,1536]{1,0:T(8,128)(2,1)S(1)}, bf16[256,1536]{1,0:T(8,128)(2,1)}, u32[]{:S(2)}) %copy-start.2) | copy-done | bytes 786456
  9.1 0.0 copy-start.3
  9.1 0.9 %copy-done.3 = f32[256,128]{1,0:T(8,128)S(1)} copy-done((f32[256,128]{1,0:T(8,128)S(1)}, f32[256,128]{1,0:T(8,128)}, u32[]{:S(2)}) %copy-start.3) | copy-done | bytes 131096
  10.0 0.0 copy-start.4
  10.0 0.9 %copy-done.4 = f32[256,128]{1,0:T(8,128)S(1)} copy-done((f32[256,128]{1,0:T(8,128)S(1)}, f32[256,128]{1,0:T(8,128)}, u32[]{:S(2)}) %copy-start.4) | copy-done | bytes 131096
  10.9 0.0 copy-start.5
  10.9 0.7 %copy-done.5 = s32[64]{0:T(128)S(1)} copy-done((s32[64]{0:T(128)S(1)}, s32[64]{0:T(128)}, u32[]{:S(2)}) %copy-start.5) | copy-done | bytes 280
  11.6 34.3 %fused_attention.1 = bf16[256,768]{1,0:T(8,128)(2,1)S(1)} custom-call(s32[1]{0:T(128)S(6)} %copy.14.ids, s32[64]{0:T(128)S(1)} %copy-done.5, s32[1]{0:T(128)S(6)} %copy.13.lengths, bf16[256,1536]{1,0:T(8,128)(2,1)S(1)} %copy-done.2, bf16[3072,768]{1,0:T(8,128)(2,1)S(1)} %copy-done, bf16[3072,256]{1,0:T(8,128)(2,1)S(1)} %copy-done.1, ...), custom_call_target="tpu_custom_call" | custom-call | tf_op jit(solution)/shard_map/fused_attention/pallas_call | solution.py:449
  45.9 0.7 %copy.15 = bf16[256,768]{1,0:T(8,128)(2,1)} copy(bf16[256,768]{1,0:T(8,128)(2,1)S(1)} %fused_attention.1) | data formatting | bytes 786432
Async XLA Ops:
  4.2 2.3 %copy-start = (bf16[3072,768]{1,0:T(8,128)(2,1)S(1)}, bf16[3072,768]{1,0:T(8,128)(2,1)}, u32[]{:S(2)}) copy-start(bf16[3072,768]{1,0:T(8,128)(2,1)} %wq.1) | copy-start | bytes 14155780
  6.5 1.4 %copy-start.1 = (bf16[3072,256]{1,0:T(8,128)(2,1)S(1)}, bf16[3072,256]{1,0:T(8,128)(2,1)}, u32[]{:S(2)}) copy-start(bf16[3072,256]{1,0:T(8,128)(2,1)} %wkv.1) | copy-start | bytes 4718596
  8.0 1.1 %copy-start.2 = (bf16[256,1536]{1,0:T(8,128)(2,1)S(1)}, bf16[256,1536]{1,0:T(8,128)(2,1)}, u32[]{:S(2)}) copy-start(bf16[256,1536]{1,0:T(8,128)(2,1)} %states.1) | copy-start | bytes 2359300
  9.1 0.9 %copy-start.3 = (f32[256,128]{1,0:T(8,128)S(1)}, f32[256,128]{1,0:T(8,128)}, u32[]{:S(2)}) copy-start(f32[256,128]{1,0:T(8,128)} %constant.4.clone.cosine) | copy-start | bytes 393220
  10.0 0.9 %copy-start.4 = (f32[256,128]{1,0:T(8,128)S(1)}, f32[256,128]{1,0:T(8,128)}, u32[]{:S(2)}) copy-start(f32[256,128]{1,0:T(8,128)} %constant.5.clone.sine) | copy-start | bytes 393220
  10.9 0.7 %copy-start.5 = (s32[64]{0:T(128)S(1)}, s32[64]{0:T(128)}, u32[]{:S(2)}) copy-start(s32[64]{0:T(128)} %slots.1) | copy-start | bytes 772

commit v2 on v1

--- a/solution.py
+++ b/solution.py
@@ -131,22 +131,26 @@
     states,
     wq,
     wkv,
-    rows,
-    cosine,
-    sine,
+    down_rows,
+    query_rows,
+    pair_rows,
+    trig,
     out,
     own_st,
     other_st,
     w_own,
     w_other,
     total,
-    plane,
+    plane_down,
+    plane_up,
+    cosine,
+    sine,
     ids_own,
     ids_in,
-    leaving,
-    landed,
-    down,
-    ups,
+    leave_down,
+    leave_up,
+    land_down,
+    land_up,
     mid_out,
     mid_in,
     kv_own,
@@ -177,7 +181,8 @@
     q_cols = wq.shape[1]
     tokens = own_st.shape[0]
     step = tokens // PIECES
-    mine = rows.shape[1]
+    mine, rank, lanes = plane_down.shape[1] // per_plane, plane_up.shape[1], plane_down.shape[3]
+    parts = plane_down.shape[0]
     core_peer = r + 1 - 2 * (r % 2)
     y_peer = r + 2 - 4 * ((r // 2) % 2)
     z_peers = [(r + per_plane * d) % count for d in range(1, planes)]
@@ -200,7 +205,15 @@
         pltpu.make_async_copy(wkv.at[own_rows], w_own.at[:, q_cols:], local_sem.at[2]),
         pltpu.make_async_copy(wq.at[other_rows], w_other.at[:, :q_cols], local_sem.at[3]),
         pltpu.make_async_copy(wkv.at[other_rows], w_other.at[:, q_cols:], local_sem.at[4]),
-        pltpu.make_async_copy(rows, plane.at[:, place(r)], local_sem.at[5]),
+        pltpu.make_async_copy(trig.at[0], cosine, local_sem.at[5]),
+        pltpu.make_async_copy(trig.at[1], sine, local_sem.at[6]),
+        pltpu.make_async_copy(query_rows, plane_up.at[place(r), :, :q_cols], local_sem.at[7]),
+        pltpu.make_async_copy(pair_rows, plane_up.at[place(r), :, q_cols:], local_sem.at[8]),
+    ] + [
+        pltpu.make_async_copy(
+            down_rows.at[:, :, pl.ds(k * lanes, lanes)], plane_down.at[k, place(r)], local_sem.at[9 + k]
+        )
+        for k in range(parts)
     ]
     for copy in loads:
         copy.start()
@@ -227,39 +240,54 @@
         )
         for p in range(PIECES)
     ]
-    y_copies = [
-        remote(rows.at[k], plane.at[k, place(r)], y_send.at[k], y_recv.at[k], {"req": y_peer})
-        for k in range(4)
-    ]
-    c_copies = [
-        remote(rows.at[k], plane.at[k, place(r)], c_send.at[k], c_recv.at[k], {"req": core_peer})
-        for k in range(4)
-    ]
+    def share(peer, send, recv):
+        made = [
+            remote(
+                down_rows.at[:, :, pl.ds(k * lanes, lanes)],
+                plane_down.at[k, place(r)],
+                send.at[k],
+                recv.at[k],
+                {"req": peer},
+            )
+            for k in range(parts)
+        ]
+        for n, (source, columns) in enumerate(
+            ((query_rows, pl.ds(0, q_cols)), (pair_rows, pl.ds(q_cols, plane_up.shape[2] - q_cols)))
+        ):
+            made.append(
+                remote(
+                    source,
+                    plane_up.at[place(r), :, columns],
+                    send.at[parts + n],
+                    recv.at[parts + n],
+                    {"req": peer},
+                )
+            )
+        return made
+
+    y_copies = share(y_peer, y_send, y_recv)
+    c_copies = share(core_peer, c_send, c_recv)
     f_copies = [
-        remote(
-            plane.at[k, place(y_peer)],
-            plane.at[k, place(y_peer)],
-            f_send.at[k],
-            f_recv.at[k],
-            {"req": core_peer},
+        remote(block, block, f_send.at[k], f_recv.at[k], {"req": core_peer})
+        for k, block in enumerate(
+            [plane_down.at[k, place(y_peer)] for k in range(parts)] + [plane_up.at[place(y_peer)]]
         )
-        for k in range(4)
     ]
     for copy in id_copies:
         copy.start()
-    for k in range(4):
-        st_copies[k].start()
+    for k in range(parts + 2):
+        if k < PIECES:
+            st_copies[k].start()
         y_copies[k].start()
         c_copies[k].start()
 
     for n in (0, 1, 2):
         loads[n].wait()
     total[...] = jnp.dot(own_st[...], w_own[...], preferred_element_type=jnp.float32)
-    loads[5].wait()
+    for copy in loads[3:]:
+        copy.wait()
     for copy in id_copies:
         copy.wait_recv()
-    loads[3].wait()
-    loads[4].wait()
 
     def add_piece(p):
         st_copies[p].wait_recv()
@@ -267,74 +295,81 @@
         total[span] += jnp.dot(other_st[span], w_other[...], preferred_element_type=jnp.float32)
 
     z_copies = []
-    selves = []
-    for k in range(4):
-        y_copies[k].wait_recv()
+
+    def stage(k):
+        up = k == parts
+        source = plane_up if up else plane_down.at[k]
+        which = (parts, parts + 1) if up else (k,)
+        for n in which:
+            y_copies[n].wait_recv()
         f_copies[k].start()
-        c_copies[k].wait_recv()
+        for n in which:
+            c_copies[n].wait_recv()
         f_copies[k].wait_recv()
 
-        def pick(j, sums, k=k):
-            record = plane[k, j]
+        def pick(j, sums):
+            record = source[j]
             made = []
             for d in range(planes):
                 wanted = ids_own[...] if d == 0 else ids_in[planes - 1 - d]
                 flag = jnp.where(wanted == base + j, 1.0, 0.0).astype(jnp.bfloat16)
+                flag = jnp.concatenate([flag] * (record.shape[0] // flag.shape[0]), axis=0)
                 flag = jnp.concatenate([flag] * (record.shape[1] // flag.shape[1]), axis=1)
                 made.append(sums[d] + flag * record)
             return tuple(made)
 
-        zero = jnp.zeros(plane.shape[2:], jnp.bfloat16)
+        zero = jnp.zeros(source.shape[1:], jnp.bfloat16)
         sums = lax.fori_loop(0, per_plane * mine, pick, (zero,) * planes)
+        leave = leave_up if up else leave_down.at[k]
+        land = land_up if up else land_down.at[k]
         for d in range(1, planes):
-            leaving[k, d - 1] = sums[d]
-        ups[k] = sums[0]
+            leave[d - 1] = sums[d]
         sent = [
-            remote(
-                leaving.at[k, d],
-                landed.at[k, d],
-                z_send.at[k, d],
-                z_recv.at[k, d],
-                {"req": peer},
-            )
+            remote(leave.at[d], land.at[d], z_send.at[k, d], z_recv.at[k, d], {"req": peer})
             for d, peer in enumerate(z_peers)
         ]
         for copy in sent:
             copy.start()
         z_copies.append(sent)
-        if k in (1, 3):
-            add_piece(k // 2)
-
-    def take(k):
+        return sums[0]
+
+    def take(k, record):
         for copy in z_copies[k]:
             copy.wait_recv()
-        record = ups[k]
+        land = land_up if k == parts else land_down.at[k]
         for d in range(planes - 1):
-            record = record + landed[k, d]
+            record = record + land[d]
         return record
 
-    rank = down.shape[0] // 2
-    wide = plane.shape[3]
-    left = half - wide
-    down[0:rank, 0:wide] = take(0)
-    down[rank:, 0:wide] = take(1)
-    tail = take(2)
-    down[0:rank, wide:] = tail[:, :left]
-    down[rank:, wide:] = tail[:, left:]
-    mid_out[...] = lax.dot_general(
-        down[...], own_st[...], (((1,), (1,)), ((), ())), preferred_element_type=jnp.float32
-    )
+    def lower(k, record):
+        part = lax.dot_general(
+            take(k, record),
+            own_st[:, k * lanes : (k + 1) * lanes],
+            (((1,), (1,)), ((), ())),
+            preferred_element_type=jnp.float32,
+        )
+        mid_out[...] = part if k == 0 else mid_out[...] + part
+
+    held = None
+    for k in range(parts):
+        fresh = stage(k)
+        if k:
+            lower(k - 1, held)
+        held = fresh
+        if k == 1:
+            add_piece(0)
+    held_up = stage(parts)
+    lower(parts - 1, held)
     mid_copy = remote(mid_out, mid_in, m_send.at[0], m_recv.at[0], {"tp": across})
     mid_copy.start()
-    up = take(3)
-    col = lax.broadcasted_iota(jnp.int32, (rank, wide), 1)
-    empty = jnp.zeros_like(up)
-    lifted = jnp.concatenate([jnp.where(col < q_cols, up, empty), jnp.where(col < q_cols, empty, up)], axis=0)
+    add_piece(1)
     add_piece(2)
+    up = take(parts, held_up)
     mid_copy.wait_recv()
     mid = jnp.transpose(mid_out[...] + mid_in[...]).astype(jnp.bfloat16)
-    extra = 0.5 * jnp.dot(mid, lifted, preferred_element_type=jnp.float32)
-    total[...] += extra
+    total[:, q_cols:] += 0.5 * jnp.dot(
+        mid[:, rank:], up[:, q_cols:], preferred_element_type=jnp.float32
+    )
 
     kv_copies = []
     keep = pl.ds(pl.multiple_of(tp * HEAD_DIM, HEAD_DIM), HEAD_DIM)
@@ -350,6 +385,9 @@
         copy.start()
         kv_copies.append(copy)
 
+    total[:, :q_cols] += 0.5 * jnp.dot(
+        mid[:, :rank], up[:, :q_cols], preferred_element_type=jnp.float32
+    )
     scale = 1.0 / math.sqrt(HEAD_DIM)
     length = lengths[0]
 
@@ -407,10 +445,9 @@
     angle = position[:, None] * inverse[None, :].astype(np.float32)
     cosine = np.cos(angle)
     sine = np.sin(angle)
-    return (
-        np.concatenate([cosine, cosine], axis=1).astype(np.float32),
-        np.concatenate([-sine, sine], axis=1).astype(np.float32),
-    )
+    return np.stack(
+        [np.concatenate([cosine, cosine], axis=1), np.concatenate([-sine, sine], axis=1)]
+    ).astype(np.float32)
 
 
 def local_fused(
@@ -430,16 +467,10 @@
     kv_cols = key_value_weight.shape[1]
     cols = q_cols + kv_cols
     mine, rank = query_up_store.shape[:2]
-    turned = jnp.transpose(down_store, (0, 2, 1))
-    rows = jnp.stack(
-        [
-            turned[:, :rank, :cols],
-            turned[:, rank:, :cols],
-            jnp.concatenate([turned[:, :rank, cols:], turned[:, rank:, cols:]], axis=2),
-            jnp.concatenate([query_up_store, key_value_store], axis=2),
-        ]
-    )
-    cosine, sine = tables(tokens)
+    down_rows = jnp.transpose(down_store, (0, 2, 1))
+    parts = 3
+    lanes = half // parts
+    trig = tables(tokens)
     peers = planes - 1
     vmem = pl.BlockSpec(memory_space=pltpu.VMEM)
     smem = pl.BlockSpec(memory_space=pltpu.SMEM)
@@ -449,7 +480,7 @@
     return pl.pallas_call(
         functools.partial(fused, planes),
         out_shape=jax.ShapeDtypeStruct((tokens, q_cols), bf16),
-        in_specs=[smem, smem, smem, hbm, hbm, hbm, hbm, vmem, vmem],
+        in_specs=[smem] * 3 + [hbm] * 7,
         out_specs=vmem,
         scratch_shapes=[
             pltpu.VMEM((tokens, half), bf16),
@@ -457,40 +488,54 @@
             pltpu.VMEM((half, cols), bf16),
             pltpu.VMEM((half, cols), bf16),
             pltpu.VMEM((tokens, cols), f32),
-            pltpu.VMEM((4, 4 * mine, rank, cols), bf16),
+            pltpu.VMEM((parts, 4 * mine, 2 * rank, lanes), bf16),
+            pltpu.VMEM((4 * mine, rank, cols), bf16),
+            pltpu.VMEM((tokens, HEAD_DIM), f32),
+            pltpu.VMEM((tokens, HEAD_DIM), f32),
             pltpu.VMEM((16, 128), jnp.int32),
             pltpu.VMEM((peers, 16, 128), jnp.int32),
-            pltpu.VMEM((4, peers, rank, cols), bf16),
-            pltpu.VMEM((4, peers, rank, cols), bf16),
-            pltpu.VMEM((2 * rank, half), bf16),
-            pltpu.VMEM((4, rank, cols), bf16),
+            pltpu.VMEM((parts, peers, 2 * rank, lanes), bf16),
+            pltpu.VMEM((peers, rank, cols), bf16),
+            pltpu.VMEM((parts, peers, 2 * rank, lanes), bf16),
+            pltpu.VMEM((peers, rank, cols), bf16),
             pltpu.VMEM((2 * rank, tokens), f32),
             pltpu.VMEM((2 * rank, tokens), f32),
             pltpu.VMEM((tokens, kv_cols), bf16),
             pltpu.VMEM((tokens, HEAD_DIM), bf16),
-            dma((6,)),
+            dma((9 + parts,)),
             dma((PIECES,)),
             dma((PIECES,)),
-            dma((4,)),
-            dma((4,)),
-            dma((4,)),
-            dma((4,)),
-            dma((4,)),
-            dma((4,)),
+            dma((parts + 2,)),
+            dma((parts + 2,)),
+            dma((parts + 2,)),
+            dma((parts + 2,)),
+            dma((parts + 1,)),
+            dma((parts + 1,)),
             dma((peers,)),
             dma((peers,)),
-            dma((4, peers)),
-            dma((4, peers)),
+            dma((parts + 1, peers)),
+            dma((parts + 1, peers)),
             dma((1,)),
             dma((1,)),
             dma((len(GROUPS),)),
             dma((len(GROUPS),)),
         ],
         compiler_params=pltpu.CompilerParams(
-            collective_id=0, has_side_effects=True, vmem_limit_bytes=40 * 1024 * 1024
+            collective_id=0, has_side_effects=True, vmem_limit_bytes=60 * 1024 * 1024
         ),
         name="fused_attention",
-    )(adapter_ids, adapter_slot, lengths, states, query_weight, key_value_weight, rows, cosine, sine)
+    )(
+        adapter_ids,
+        adapter_slot,
+        lengths,
+        states,
+        query_weight,
+        key_value_weight,
+        down_rows,
+        query_up_store,
+        key_value_store,
+        trig,
+    )
 
 
 def solution(mesh):

time: 47 us -> 38.1 us (0.81)
  local copies, waits for them, and re-layouts: 8.96 us -> 1.77 us
  other arithmetic: 2.01 us -> 0 us
  Pallas kernels: 34.3 us -> 34.9 us
    unnamed x13 -> x1, local copies, waits for them, and re-layouts: 8.08 us -> 1.77 us
    another operation x3 -> x0, other arithmetic: 2.01 us -> none  [local_fused(): jnp.stack([turned[:, :rank, :cols], turned[:, rank:, :cols], jnp.concaten...]
    slice x1 -> x0, local copies, waits for them, and re-layouts: 0.88 us -> none  [local_fused(): turned[:, :rank, cols:]]
    pallas_call x1, Pallas kernels: 34.3 us -> 34.9 us  [local_fused(): pl.pallas_call(functools.partial(fused, planes), out_shape=jax.ShapeDtype...]
where the time goes in v2:
time: 38.1 us; the launch traced here: 38 us
  Pallas kernels  34.9 us (92%)
  local copies, waits for them, and re-layouts  1.77 us (5%)
  between operations  1.3 us (3%)
    pallas_call x1, Pallas kernels, local_fused(): pl.pallas_call(functools.partial(fused, planes), out_shape=jax.ShapeDtype...  34.9 us
    unnamed x1, local copies, waits for them, and re-layouts  1.77 us

profile of v2, /device:TPU:0, one launch (start us, length us, event | category | flops | bytes accessed | tf_op | source)
XLA Modules:
  0.0 38.0 jit_solution(4631083942585289332)
XLA Ops:
  1.3 34.9 %fused_attention.1 = bf16[256,768]{1,0:T(8,128)(2,1)} custom-call(s32[1]{0:T(128)S(6)} %copy.13.ids, s32[64]{0:T(128)} %slots.1, s32[1]{0:T(128)S(6)} %copy.12.lengths, bf16[256,1536]{1,0:T(8,128)(2,1)} %states.1, bf16[3072,768]{1,0:T(8,128)(2,1)} %wq.1, bf16[3072,256]{1,0:T(8,128)(2,1)} %wkv.1, bf16[4,32,1536]{2,1,0:T(8,128)(2,1)} %bitcast.1, ...), custom_call_target="tpu_custom_call" | custom-call | tf_op jit(solution)/shard_map/fused_attention/pallas_call | solution.py:480
  36.2 1.8 %copy.14 = bf16[256,768]{1,0:T(8,128)(2,1)} copy(bf16[256,768]{1,0:T(8,128)(2,1)} %fused_attention.1) | data formatting | bytes 786432

commit v3 on v2

--- a/solution.py
+++ b/solution.py
@@ -276,7 +276,7 @@
     for copy in id_copies:
         copy.start()
     for k in range(parts + 2):
-        if k < PIECES:
+        if k < PIECES - 1:
             st_copies[k].start()
         y_copies[k].start()
         c_copies[k].start()
@@ -289,10 +289,11 @@
     for copy in id_copies:
         copy.wait_recv()
 
-    def add_piece(p):
-        st_copies[p].wait_recv()
+    def add_piece(p, columns=slice(None)):
         span = pl.ds(p * step, step)
-        total[span] += jnp.dot(other_st[span], w_other[...], preferred_element_type=jnp.float32)
+        total[span, columns] += jnp.dot(
+            other_st[span], w_other[:, columns], preferred_element_type=jnp.float32
+        )
 
     z_copies = []
 
@@ -356,13 +357,15 @@
         if k:
             lower(k - 1, held)
         held = fresh
-        if k == 1:
-            add_piece(0)
+        if k in (2, 5):
+            st_copies[k // 3].wait_recv()
+            add_piece(k // 3)
     held_up = stage(parts)
     lower(parts - 1, held)
     mid_copy = remote(mid_out, mid_in, m_send.at[0], m_recv.at[0], {"tp": across})
     mid_copy.start()
-    add_piece(1)
+    st_copies[PIECES - 1].start()
+    st_copies[2].wait_recv()
     add_piece(2)
     up = take(parts, held_up)
     mid_copy.wait_recv()
@@ -371,13 +374,19 @@
         mid[:, rank:], up[:, q_cols:], preferred_element_type=jnp.float32
     )
 
-    kv_copies = []
     keep = pl.ds(pl.multiple_of(tp * HEAD_DIM, HEAD_DIM), HEAD_DIM)
     give = pl.ds(pl.multiple_of(across * HEAD_DIM, HEAD_DIM), HEAD_DIM)
-    for g, (first, size) in enumerate(GROUPS):
-        if g == 1:
-            add_piece(3)
-        span = pl.ds(first, size)
+    scale = 1.0 / math.sqrt(HEAD_DIM)
+    length = lengths[0]
+    kv_copies = []
+    key_parts = []
+    value_parts = []
+
+    def turn(x, span):
+        return (x * cosine[span] + pltpu.roll(x, HEAD_DIM // 2, 1) * sine[span]).astype(jnp.bfloat16)
+
+    def swap(g):
+        span = pl.ds(*GROUPS[g])
         kv_own[span] = total[span, q_cols:].astype(jnp.bfloat16)
         copy = remote(
             kv_own.at[span, give], kv_in.at[span], kv_send.at[g], kv_recv.at[g], {"tp": across}
@@ -385,23 +394,17 @@
         copy.start()
         kv_copies.append(copy)
 
-    total[:, :q_cols] += 0.5 * jnp.dot(
-        mid[:, :rank], up[:, :q_cols], preferred_element_type=jnp.float32
-    )
-    scale = 1.0 / math.sqrt(HEAD_DIM)
-    length = lengths[0]
-
-    def turn(x, span):
-        return (x * cosine[span] + pltpu.roll(x, HEAD_DIM // 2, 1) * sine[span]).astype(jnp.bfloat16)
-
-    key_parts = []
-    value_parts = []
-    for g, (first, size) in enumerate(GROUPS):
+    def attend(g):
+        first, size = GROUPS[g]
         span = pl.ds(first, size)
         turned = [
             turn(total[span, h * HEAD_DIM : (h + 1) * HEAD_DIM], span)
             for h in range(q_cols // HEAD_DIM)
         ]
+        reach = first + size
+        row = lax.broadcasted_iota(jnp.int32, (size, reach), 0) + first
+        column = lax.broadcasted_iota(jnp.int32, (size, reach), 1)
+        allowed = (column <= row) & (column < length)
         kv_copies[g].wait_recv()
         kept = kv_own[span, keep]
         came = kv_in[span]
@@ -410,24 +413,29 @@
         value = jnp.where(first_side, came.astype(jnp.float32), kept.astype(jnp.float32))
         key_parts.append(turn(key, span))
         value_parts.append(value.astype(jnp.bfloat16))
-        reach = first + size
-        keys = jnp.concatenate(key_parts, axis=0) if g else key_parts[0]
-        values = jnp.concatenate(value_parts, axis=0) if g else value_parts[0]
-        row = lax.broadcasted_iota(jnp.int32, (size, reach), 0) + first
-        column = lax.broadcasted_iota(jnp.int32, (size, reach), 1)
-        allowed = (column <= row) & (column < length)
-        live = lax.broadcasted_iota(jnp.int32, (size, HEAD_DIM), 0) + first < length
+        keys = jnp.concatenate(key_parts, axis=0)
+        values = jnp.concatenate(value_parts, axis=0)
         for h, query in enumerate(turned):
             scores = lax.dot_general(
                 query, keys, (((1,), (1,)), ((), ())), preferred_element_type=jnp.float32
             )
             scores = jnp.where(allowed, scores * scale, -jnp.inf)
             expo = jnp.exp(scores - jnp.max(scores, axis=1, keepdims=True))
-            weights = (expo / jnp.sum(expo, axis=1, keepdims=True)).astype(jnp.bfloat16)
+            share_of = 1.0 / jnp.sum(expo, axis=1, keepdims=True)
+            weights = (expo * share_of).astype(jnp.bfloat16)
             mixed = jnp.dot(weights, values, preferred_element_type=jnp.float32)
-            out[span, h * HEAD_DIM : (h + 1) * HEAD_DIM] = jnp.where(live, mixed, 0.0).astype(
-                jnp.bfloat16
-            )
+            out[span, h * HEAD_DIM : (h + 1) * HEAD_DIM] = mixed.astype(jnp.bfloat16)
+
+    swap(0)
+    total[:, :q_cols] += 0.5 * jnp.dot(
+        mid[:, :rank], up[:, :q_cols], preferred_element_type=jnp.float32
+    )
+    attend(0)
+    st_copies[PIECES - 1].wait_recv()
+    add_piece(PIECES - 1, slice(q_cols, None))
+    swap(1)
+    add_piece(PIECES - 1, slice(0, q_cols))
+    attend(1)
 
     for copy in id_copies + st_copies + y_copies + c_copies + f_copies + [mid_copy] + kv_copies:
         copy.wait_send()
@@ -468,7 +476,7 @@
     cols = q_cols + kv_cols
     mine, rank = query_up_store.shape[:2]
     down_rows = jnp.transpose(down_store, (0, 2, 1))
-    parts = 3
+    parts = 6
     lanes = half // parts
     trig = tables(tokens)
     peers = planes - 1
@@ -477,7 +485,7 @@
     hbm = pl.BlockSpec(memory_space=pl.ANY)
     bf16, f32 = jnp.bfloat16, jnp.float32
     dma = pltpu.SemaphoreType.DMA
-    return pl.pallas_call(
+    context = pl.pallas_call(
         functools.partial(fused, planes),
         out_shape=jax.ShapeDtypeStruct((tokens, q_cols), bf16),
         in_specs=[smem] * 3 + [hbm] * 7,
@@ -536,6 +544,8 @@
         key_value_store,
         trig,
     )
+    live = lax.broadcasted_iota(jnp.int32, context.shape, 0) < lengths[0]
+    return jnp.where(live, context, jnp.zeros_like(context))
 
 
 def solution(mesh):

time: 38.1 us -> 46.6 us (1.22)
  Pallas kernels: 34.9 us -> 43.2 us
  other arithmetic: 0 us -> 1.85 us
  local copies, waits for them, and re-layouts: 1.77 us -> 0 us
    pallas_call x1, Pallas kernels: 34.9 us -> 43.2 us  [local_fused(): pl.pallas_call(functools.partial(fused, planes), out_shape=jax.ShapeDtype...]
    select_n x0 -> x1, other arithmetic: none -> 1.85 us  [local_fused(): return jnp.where(live, context, jnp.zeros_like(context))]
    unnamed x1 -> x0, local copies, waits for them, and re-layouts: 1.77 us -> none
where the time goes in v3:
time: 46.6 us; the launch traced here: 46.4 us
  Pallas kernels  43.2 us (93%)
  other arithmetic  1.85 us (4%)
  between operations  1.31 us (3%)
    pallas_call x1, Pallas kernels, local_fused(): pl.pallas_call(functools.partial(fused, planes), out_shape=jax.ShapeDtype...  43.2 us
    select_n x1, other arithmetic, local_fused(): return jnp.where(live, context, jnp.zeros_like(context))  1.85 us

profile of v3, /device:TPU:0, one launch (start us, length us, event | category | flops | bytes accessed | tf_op | source)
XLA Modules:
  0.0 46.4 jit_solution(18246428332135267743)
XLA Ops:
  1.3 43.2 %fused_attention.1 = bf16[256,768]{1,0:T(8,128)(2,1)} custom-call(s32[1]{0:T(128)S(6)} %copy.12.ids, s32[64]{0:T(128)} %slots.1, s32[1]{0:T(128)} %copy.11.lengths, bf16[256,1536]{1,0:T(8,128)(2,1)} %states.1, bf16[3072,768]{1,0:T(8,128)(2,1)} %wq.1, bf16[3072,256]{1,0:T(8,128)(2,1)} %wkv.1, bf16[4,32,1536]{2,1,0:T(8,128)(2,1)} %bitcast.3, ...), custom_call_target="tpu_custom_call" | custom-call | tf_op jit(solution)/shard_map/fused_attention/pallas_call | solution.py:488
  44.6 1.8 %broadcast_select_fusion = bf16[256,768]{1,0:T(8,128)(2,1)} fusion(bf16[256,768]{1,0:T(8,128)(2,1)} %fused_attention.1, pred[256]{0:T(512)(128)(4,1)S(1)} %iota_compare_fusion), kind=kLoop, calls=%fused_computation | loop fusion | flops 196608 | bytes 786688 | tf_op jit(solution)/shard_map/jit(_where)/select_n | solution.py:548
  (1 shorter events, 0.0 us)

commit v4 on v3

--- a/solution.py
+++ b/solution.py
@@ -147,6 +147,7 @@
     sine,
     ids_own,
     ids_in,
+    flags,
     leave_down,
     leave_up,
     land_down,
@@ -181,8 +182,8 @@
     q_cols = wq.shape[1]
     tokens = own_st.shape[0]
     step = tokens // PIECES
-    mine, rank, lanes = plane_down.shape[1] // per_plane, plane_up.shape[1], plane_down.shape[3]
-    parts = plane_down.shape[0]
+    mine, rank, lanes = plane_up.shape[0] // per_plane, plane_up.shape[1], land_down.shape[3]
+    parts = land_down.shape[0]
     core_peer = r + 1 - 2 * (r % 2)
     y_peer = r + 2 - 4 * ((r // 2) % 2)
     z_peers = [(r + per_plane * d) % count for d in range(1, planes)]
@@ -209,11 +210,7 @@
         pltpu.make_async_copy(trig.at[1], sine, local_sem.at[6]),
         pltpu.make_async_copy(query_rows, plane_up.at[place(r), :, :q_cols], local_sem.at[7]),
         pltpu.make_async_copy(pair_rows, plane_up.at[place(r), :, q_cols:], local_sem.at[8]),
-    ] + [
-        pltpu.make_async_copy(
-            down_rows.at[:, :, pl.ds(k * lanes, lanes)], plane_down.at[k, place(r)], local_sem.at[9 + k]
-        )
-        for k in range(parts)
+        pltpu.make_async_copy(down_rows, plane_down.at[place(r)], local_sem.at[9]),
     ]
     for copy in loads:
         copy.start()
@@ -240,16 +237,17 @@
         )
         for p in range(PIECES)
     ]
-    def share(peer, send, recv):
+    def share(peer, send, recv, cuts):
+        wide = half // cuts
         made = [
             remote(
-                down_rows.at[:, :, pl.ds(k * lanes, lanes)],
-                plane_down.at[k, place(r)],
+                down_rows.at[:, :, pl.ds(k * wide, wide)],
+                plane_down.at[place(r), :, pl.ds(k * wide, wide)],
                 send.at[k],
                 recv.at[k],
                 {"req": peer},
             )
-            for k in range(parts)
+            for k in range(cuts)
         ]
         for n, (source, columns) in enumerate(
             ((query_rows, pl.ds(0, q_cols)), (pair_rows, pl.ds(q_cols, plane_up.shape[2] - q_cols)))
@@ -258,28 +256,26 @@
                 remote(
                     source,
                     plane_up.at[place(r), :, columns],
-                    send.at[parts + n],
-                    recv.at[parts + n],
+                    send.at[cuts + n],
+                    recv.at[cuts + n],
                     {"req": peer},
                 )
             )
         return made
 
-    y_copies = share(y_peer, y_send, y_recv)
-    c_copies = share(core_peer, c_send, c_recv)
+    y_copies = share(y_peer, y_send, y_recv, parts)
+    c_copies = share(core_peer, c_send, c_recv, 1)
     f_copies = [
         remote(block, block, f_send.at[k], f_recv.at[k], {"req": core_peer})
         for k, block in enumerate(
-            [plane_down.at[k, place(y_peer)] for k in range(parts)] + [plane_up.at[place(y_peer)]]
+            [plane_down.at[place(y_peer), :, pl.ds(k * lanes, lanes)] for k in range(parts)]
+            + [plane_up.at[place(y_peer)]]
         )
     ]
-    for copy in id_copies:
+    y_copies[0].start()
+    st_copies[0].start()
+    for copy in id_copies + y_copies[1:] + c_copies + st_copies[1:]:
         copy.start()
-    for k in range(parts + 2):
-        if k < PIECES - 1:
-            st_copies[k].start()
-        y_copies[k].start()
-        c_copies[k].start()
 
     for n in (0, 1, 2):
         loads[n].wait()
@@ -297,34 +293,39 @@
 
     z_copies = []
 
+    for d in range(planes):
+        wanted = ids_own[...] if d == 0 else ids_in[planes - 1 - d]
+        for j in range(per_plane * mine):
+            flags[d, j] = jnp.where(wanted == base + j, 1.0, 0.0).astype(jnp.bfloat16)
+
+    def forward(k):
+        for n in (parts, parts + 1) if k == parts else (k,):
+            y_copies[n].wait_recv()
+        f_copies[k].start()
+
     def stage(k):
         up = k == parts
-        source = plane_up if up else plane_down.at[k]
-        which = (parts, parts + 1) if up else (k,)
-        for n in which:
-            y_copies[n].wait_recv()
-        f_copies[k].start()
-        for n in which:
-            c_copies[n].wait_recv()
+        if up or k == 0:
+            for copy in c_copies[1:] if up else c_copies[:1]:
+                copy.wait_recv()
         f_copies[k].wait_recv()
-
-        def pick(j, sums):
-            record = source[j]
-            made = []
-            for d in range(planes):
-                wanted = ids_own[...] if d == 0 else ids_in[planes - 1 - d]
-                flag = jnp.where(wanted == base + j, 1.0, 0.0).astype(jnp.bfloat16)
-                flag = jnp.concatenate([flag] * (record.shape[0] // flag.shape[0]), axis=0)
-                flag = jnp.concatenate([flag] * (record.shape[1] // flag.shape[1]), axis=1)
-                made.append(sums[d] + flag * record)
-            return tuple(made)
-
-        zero = jnp.zeros(source.shape[1:], jnp.bfloat16)
-        sums = lax.fori_loop(0, per_plane * mine, pick, (zero,) * planes)
+        kept = []
         leave = leave_up if up else leave_down.at[k]
         land = land_up if up else land_down.at[k]
-        for d in range(1, planes):
-            leave[d - 1] = sums[d]
+        for top in range(0, land.shape[1], 16):
+            sums = [None] * planes
+            for j in range(per_plane * mine):
+                if up:
+                    record = plane_up[j, top : top + 16]
+                else:
+                    record = plane_down[j, top : top + 16, k * lanes : (k + 1) * lanes]
+                for d in range(planes):
+                    flag = flags[d, j]
+                    flag = jnp.concatenate([flag] * (record.shape[1] // flag.shape[1]), axis=1)
+                    sums[d] = flag * record if j == 0 else sums[d] + flag * record
+            for d in range(1, planes):
+                leave[d - 1, top : top + 16] = sums[d]
+            kept.append(sums[0])
         sent = [
             remote(leave.at[d], land.at[d], z_send.at[k, d], z_recv.at[k, d], {"req": peer})
             for d, peer in enumerate(z_peers)
@@ -332,7 +333,7 @@
         for copy in sent:
             copy.start()
         z_copies.append(sent)
-        return sums[0]
+        return jnp.concatenate(kept, axis=0)
 
     def take(k, record):
         for copy in z_copies[k]:
@@ -351,22 +352,25 @@
         )
         mid_out[...] = part if k == 0 else mid_out[...] + part
 
-    held = None
-    for k in range(parts):
-        fresh = stage(k)
-        if k:
-            lower(k - 1, held)
-        held = fresh
-        if k in (2, 5):
-            st_copies[k // 3].wait_recv()
-            add_piece(k // 3)
+    held = []
+    forward(0)
+    forward(1)
+    held.append(stage(0))
+    forward(2)
+    held.append(stage(1))
+    lower(0, held[0])
+    held.append(stage(2))
+    st_copies[0].wait_recv()
+    add_piece(0)
+    lower(1, held[1])
+    forward(parts)
     held_up = stage(parts)
-    lower(parts - 1, held)
+    lower(2, held[2])
     mid_copy = remote(mid_out, mid_in, m_send.at[0], m_recv.at[0], {"tp": across})
     mid_copy.start()
-    st_copies[PIECES - 1].start()
-    st_copies[2].wait_recv()
-    add_piece(2)
+    for p in (1, 2):
+        st_copies[p].wait_recv()
+        add_piece(p)
     up = take(parts, held_up)
     mid_copy.wait_recv()
     mid = jnp.transpose(mid_out[...] + mid_in[...]).astype(jnp.bfloat16)
@@ -405,6 +409,7 @@
         row = lax.broadcasted_iota(jnp.int32, (size, reach), 0) + first
         column = lax.broadcasted_iota(jnp.int32, (size, reach), 1)
         allowed = (column <= row) & (column < length)
+        live = lax.broadcasted_iota(jnp.int32, (size, HEAD_DIM), 0) + first < length
         kv_copies[g].wait_recv()
         kept = kv_own[span, keep]
         came = kv_in[span]
@@ -424,17 +429,19 @@
             share_of = 1.0 / jnp.sum(expo, axis=1, keepdims=True)
             weights = (expo * share_of).astype(jnp.bfloat16)
             mixed = jnp.dot(weights, values, preferred_element_type=jnp.float32)
-            out[span, h * HEAD_DIM : (h + 1) * HEAD_DIM] = mixed.astype(jnp.bfloat16)
+            out[span, h * HEAD_DIM : (h + 1) * HEAD_DIM] = jnp.where(live, mixed, 0.0).astype(
+                jnp.bfloat16
+            )
 
     swap(0)
     total[:, :q_cols] += 0.5 * jnp.dot(
         mid[:, :rank], up[:, :q_cols], preferred_element_type=jnp.float32
     )
-    attend(0)
     st_copies[PIECES - 1].wait_recv()
     add_piece(PIECES - 1, slice(q_cols, None))
     swap(1)
     add_piece(PIECES - 1, slice(0, q_cols))
+    attend(0)
     attend(1)
 
     for copy in id_copies + st_copies + y_copies + c_copies + f_copies + [mid_copy] + kv_copies:
@@ -476,7 +483,7 @@
     cols = q_cols + kv_cols
     mine, rank = query_up_store.shape[:2]
     down_rows = jnp.transpose(down_store, (0, 2, 1))
-    parts = 6
+    parts = 3
     lanes = half // parts
     trig = tables(tokens)
     peers = planes - 1
@@ -485,7 +492,7 @@
     hbm = pl.BlockSpec(memory_space=pl.ANY)
     bf16, f32 = jnp.bfloat16, jnp.float32
     dma = pltpu.SemaphoreType.DMA
-    context = pl.pallas_call(
+    return pl.pallas_call(
         functools.partial(fused, planes),
         out_shape=jax.ShapeDtypeStruct((tokens, q_cols), bf16),
         in_specs=[smem] * 3 + [hbm] * 7,
@@ -496,12 +503,13 @@
             pltpu.VMEM((half, cols), bf16),
             pltpu.VMEM((half, cols), bf16),
             pltpu.VMEM((tokens, cols), f32),
-            pltpu.VMEM((parts, 4 * mine, 2 * rank, lanes), bf16),
+            pltpu.VMEM((4 * mine, 2 * rank, half), bf16),
             pltpu.VMEM((4 * mine, rank, cols), bf16),
             pltpu.VMEM((tokens, HEAD_DIM), f32),
             pltpu.VMEM((tokens, HEAD_DIM), f32),
             pltpu.VMEM((16, 128), jnp.int32),
             pltpu.VMEM((peers, 16, 128), jnp.int32),
+            pltpu.VMEM((planes, 4 * mine, 16, 128), bf16),
             pltpu.VMEM((parts, peers, 2 * rank, lanes), bf16),
             pltpu.VMEM((peers, rank, cols), bf16),
             pltpu.VMEM((parts, peers, 2 * rank, lanes), bf16),
@@ -510,7 +518,7 @@
             pltpu.VMEM((2 * rank, tokens), f32),
             pltpu.VMEM((tokens, kv_cols), bf16),
             pltpu.VMEM((tokens, HEAD_DIM), bf16),
-            dma((9 + parts,)),
+            dma((10,)),
             dma((PIECES,)),
             dma((PIECES,)),
             dma((parts + 2,)),
@@ -544,8 +552,6 @@
         key_value_store,
         trig,
     )
-    live = lax.broadcasted_iota(jnp.int32, context.shape, 0) < lengths[0]
-    return jnp.where(live, context, jnp.zeros_like(context))
 
 
 def solution(mesh):

time: 46.6 us -> 39.4 us (0.85)
  Pallas kernels: 43.2 us -> 36.1 us
  other arithmetic: 1.85 us -> 0 us
  local copies, waits for them, and re-layouts: 0 us -> 1.77 us
    pallas_call x1, Pallas kernels: 43.2 us -> 36.1 us  [local_fused(): pl.pallas_call(functools.partial(fused, planes), out_shape=jax.ShapeDtype...]
    select_n x1 -> x0, other arithmetic: 1.85 us -> none  [local_fused(): return jnp.where(live, context, jnp.zeros_like(context))]
    unnamed x0 -> x1, local copies, waits for them, and re-layouts: none -> 1.77 us
where the time goes in v4:
time: 39.4 us; the launch traced here: 39.2 us
  Pallas kernels  36.1 us (92%)
  local copies, waits for them, and re-layouts  1.77 us (4%)
  between operations  1.3 us (3%)
    pallas_call x1, Pallas kernels, local_fused(): pl.pallas_call(functools.partial(fused, planes), out_shape=jax.ShapeDtype...  36.1 us
    unnamed x1, local copies, waits for them, and re-layouts  1.77 us

profile of v4, /device:TPU:0, one launch (start us, length us, event | category | flops | bytes accessed | tf_op | source)
XLA Modules:
  0.0 39.2 jit_solution(14930464992768271389)
XLA Ops:
  1.3 36.1 %fused_attention.1 = bf16[256,768]{1,0:T(8,128)(2,1)} custom-call(s32[1]{0:T(128)S(6)} %copy.13.ids, s32[64]{0:T(128)} %slots.1, s32[1]{0:T(128)S(6)} %copy.12.lengths, bf16[256,1536]{1,0:T(8,128)(2,1)} %states.1, bf16[3072,768]{1,0:T(8,128)(2,1)} %wq.1, bf16[3072,256]{1,0:T(8,128)(2,1)} %wkv.1, bf16[4,32,1536]{2,1,0:T(8,128)(2,1)} %bitcast.1, ...), custom_call_target="tpu_custom_call" | custom-call | tf_op jit(solution)/shard_map/fused_attention/pallas_call | solution.py:495
  37.4 1.8 %copy.14 = bf16[256,768]{1,0:T(8,128)(2,1)} copy(bf16[256,768]{1,0:T(8,128)(2,1)} %fused_attention.1) | data formatting | bytes 786432

commit v5 on v4

--- a/solution.py
+++ b/solution.py
@@ -138,20 +138,24 @@
     out,
     own_st,
     other_st,
-    w_own,
-    w_other,
+    wq_own,
+    wkv_own,
+    wq_other,
+    wkv_other,
     total,
     plane_down,
-    plane_up,
-    cosine,
-    sine,
+    plane_q,
+    plane_kv,
+    turns,
     ids_own,
     ids_in,
     flags,
     leave_down,
-    leave_up,
+    leave_kv,
+    leave_q,
     land_down,
-    land_up,
+    land_kv,
+    land_q,
     mid_out,
     mid_in,
     kv_own,
@@ -182,8 +186,8 @@
     q_cols = wq.shape[1]
     tokens = own_st.shape[0]
     step = tokens // PIECES
-    mine, rank, lanes = plane_up.shape[0] // per_plane, plane_up.shape[1], land_down.shape[3]
-    parts = land_down.shape[0]
+    parts = plane_down.shape[0]
+    mine, rank = plane_q.shape[0] // per_plane, plane_q.shape[1]
     core_peer = r + 1 - 2 * (r % 2)
     y_peer = r + 2 - 4 * ((r // 2) % 2)
     z_peers = [(r + per_plane * d) % count for d in range(1, planes)]
@@ -202,15 +206,18 @@
     other_rows = pl.ds(pl.multiple_of(across * half, half), half)
     loads = [
         pltpu.make_async_copy(states, own_st, local_sem.at[0]),
-        pltpu.make_async_copy(wq.at[own_rows], w_own.at[:, :q_cols], local_sem.at[1]),
-        pltpu.make_async_copy(wkv.at[own_rows], w_own.at[:, q_cols:], local_sem.at[2]),
-        pltpu.make_async_copy(wq.at[other_rows], w_other.at[:, :q_cols], local_sem.at[3]),
-        pltpu.make_async_copy(wkv.at[other_rows], w_other.at[:, q_cols:], local_sem.at[4]),
-        pltpu.make_async_copy(trig.at[0], cosine, local_sem.at[5]),
-        pltpu.make_async_copy(trig.at[1], sine, local_sem.at[6]),
-        pltpu.make_async_copy(query_rows, plane_up.at[place(r), :, :q_cols], local_sem.at[7]),
-        pltpu.make_async_copy(pair_rows, plane_up.at[place(r), :, q_cols:], local_sem.at[8]),
-        pltpu.make_async_copy(down_rows, plane_down.at[place(r)], local_sem.at[9]),
+        pltpu.make_async_copy(wq.at[own_rows], wq_own, local_sem.at[1]),
+        pltpu.make_async_copy(wkv.at[own_rows], wkv_own, local_sem.at[2]),
+        pltpu.make_async_copy(wq.at[other_rows], wq_other, local_sem.at[3]),
+        pltpu.make_async_copy(wkv.at[other_rows], wkv_other, local_sem.at[4]),
+        pltpu.make_async_copy(trig, turns, local_sem.at[5]),
+        pltpu.make_async_copy(query_rows, plane_q.at[place(r)], local_sem.at[6]),
+        pltpu.make_async_copy(pair_rows, plane_kv.at[place(r)], local_sem.at[7]),
+    ] + [
+        pltpu.make_async_copy(
+            down_rows.at[:, pl.ds(k * rank, rank)], plane_down.at[k, place(r)], local_sem.at[8 + k]
+        )
+        for k in range(parts)
     ]
     for copy in loads:
         copy.start()
@@ -237,40 +244,29 @@
         )
         for p in range(PIECES)
     ]
-    def share(peer, send, recv, cuts):
-        wide = half // cuts
-        made = [
-            remote(
-                down_rows.at[:, :, pl.ds(k * wide, wide)],
-                plane_down.at[place(r), :, pl.ds(k * wide, wide)],
-                send.at[k],
-                recv.at[k],
-                {"req": peer},
-            )
-            for k in range(cuts)
+    def share(peer, send, recv):
+        ends = [
+            (down_rows.at[:, pl.ds(k * rank, rank)], plane_down.at[k, place(r)]) for k in range(parts)
+        ] + [(pair_rows, plane_kv.at[place(r)]), (query_rows, plane_q.at[place(r)])]
+        return [
+            remote(source, target, send.at[n], recv.at[n], {"req": peer})
+            for n, (source, target) in enumerate(ends)
         ]
-        for n, (source, columns) in enumerate(
-            ((query_rows, pl.ds(0, q_cols)), (pair_rows, pl.ds(q_cols, plane_up.shape[2] - q_cols)))
-        ):
-            made.append(
-                remote(
-                    source,
-                    plane_up.at[place(r), :, columns],
-                    send.at[cuts + n],
-                    recv.at[cuts + n],
-                    {"req": peer},
-                )
-            )
-        return made
-
-    y_copies = share(y_peer, y_send, y_recv, parts)
-    c_copies = share(core_peer, c_send, c_recv, 1)
+
+    planes_of = [plane_down.at[k] for k in range(parts)] + [plane_kv, plane_q]
+    leaves = [leave_down.at[k] for k in range(parts)] + [leave_kv, leave_q]
+    lands = [land_down.at[k] for k in range(parts)] + [land_kv, land_q]
+    y_copies = share(y_peer, y_send, y_recv)
+    c_copies = share(core_peer, c_send, c_recv)
     f_copies = [
-        remote(block, block, f_send.at[k], f_recv.at[k], {"req": core_peer})
-        for k, block in enumerate(
-            [plane_down.at[place(y_peer), :, pl.ds(k * lanes, lanes)] for k in range(parts)]
-            + [plane_up.at[place(y_peer)]]
-        )
+        remote(
+            block.at[place(y_peer)],
+            block.at[place(y_peer)],
+            f_send.at[k],
+            f_recv.at[k],
+            {"req": core_peer},
+        )
+        for k, block in enumerate(planes_of)
     ]
     y_copies[0].start()
     st_copies[0].start()
@@ -279,17 +275,29 @@
 
     for n in (0, 1, 2):
         loads[n].wait()
-    total[...] = jnp.dot(own_st[...], w_own[...], preferred_element_type=jnp.float32)
+    total[:, :q_cols] = jnp.dot(own_st[...], wq_own[...], preferred_element_type=jnp.float32)
+    total[:, q_cols:] = jnp.dot(own_st[...], wkv_own[...], preferred_element_type=jnp.float32)
     for copy in loads[3:]:
         copy.wait()
     for copy in id_copies:
         copy.wait_recv()
 
-    def add_piece(p, columns=slice(None)):
+    def add_q(p):
         span = pl.ds(p * step, step)
-        total[span, columns] += jnp.dot(
-            other_st[span], w_other[:, columns], preferred_element_type=jnp.float32
-        )
+        total[span, :q_cols] += jnp.dot(
+            other_st[span], wq_other[...], preferred_element_type=jnp.float32
+        )
+
+    def add_kv(p):
+        span = pl.ds(p * step, step)
+        total[span, q_cols:] += jnp.dot(
+            other_st[span], wkv_other[...], preferred_element_type=jnp.float32
+        )
+
+    def add_piece(p):
+        st_copies[p].wait_recv()
+        add_kv(p)
+        add_q(p)
 
     z_copies = []
 
@@ -299,33 +307,21 @@
             flags[d, j] = jnp.where(wanted == base + j, 1.0, 0.0).astype(jnp.bfloat16)
 
     def forward(k):
-        for n in (parts, parts + 1) if k == parts else (k,):
-            y_copies[n].wait_recv()
+        y_copies[k].wait_recv()
         f_copies[k].start()
 
     def stage(k):
-        up = k == parts
-        if up or k == 0:
-            for copy in c_copies[1:] if up else c_copies[:1]:
-                copy.wait_recv()
+        c_copies[k].wait_recv()
         f_copies[k].wait_recv()
-        kept = []
-        leave = leave_up if up else leave_down.at[k]
-        land = land_up if up else land_down.at[k]
-        for top in range(0, land.shape[1], 16):
-            sums = [None] * planes
-            for j in range(per_plane * mine):
-                if up:
-                    record = plane_up[j, top : top + 16]
-                else:
-                    record = plane_down[j, top : top + 16, k * lanes : (k + 1) * lanes]
-                for d in range(planes):
-                    flag = flags[d, j]
-                    flag = jnp.concatenate([flag] * (record.shape[1] // flag.shape[1]), axis=1)
-                    sums[d] = flag * record if j == 0 else sums[d] + flag * record
-            for d in range(1, planes):
-                leave[d - 1, top : top + 16] = sums[d]
-            kept.append(sums[0])
+        source, leave, land = planes_of[k], leaves[k], lands[k]
+        sums = [None] * planes
+        for j in range(per_plane * mine):
+            record = source[j]
+            for d in range(planes):
+                flag = jnp.concatenate([flags[d, j]] * (record.shape[1] // flags.shape[3]), axis=1)
+                sums[d] = flag * record if j == 0 else sums[d] + flag * record
+        for d in range(1, planes):
+            leave[d - 1] = sums[d]
         sent = [
             remote(leave.at[d], land.at[d], z_send.at[k, d], z_recv.at[k, d], {"req": peer})
             for d, peer in enumerate(z_peers)
@@ -333,50 +329,40 @@
         for copy in sent:
             copy.start()
         z_copies.append(sent)
-        return jnp.concatenate(kept, axis=0)
-
-    def take(k, record):
+        return sums[0]
+
+    def take(k):
         for copy in z_copies[k]:
             copy.wait_recv()
-        land = land_up if k == parts else land_down.at[k]
+        record = held[k]
         for d in range(planes - 1):
-            record = record + land[d]
+            record = record + lands[k][d]
         return record
 
-    def lower(k, record):
-        part = lax.dot_general(
-            take(k, record),
-            own_st[:, k * lanes : (k + 1) * lanes],
-            (((1,), (1,)), ((), ())),
-            preferred_element_type=jnp.float32,
-        )
-        mid_out[...] = part if k == 0 else mid_out[...] + part
+    def lower(k):
+        mid_out[k * rank : (k + 1) * rank] = lax.dot_general(
+            take(k), own_st[...], (((1,), (1,)), ((), ())), preferred_element_type=jnp.float32
+        )
 
     held = []
     forward(0)
+    held.append(stage(0))
     forward(1)
-    held.append(stage(0))
+    held.append(stage(1))
+    lower(0)
+    add_piece(0)
     forward(2)
-    held.append(stage(1))
-    lower(0, held[0])
+    forward(3)
     held.append(stage(2))
-    st_copies[0].wait_recv()
-    add_piece(0)
-    lower(1, held[1])
-    forward(parts)
-    held_up = stage(parts)
-    lower(2, held[2])
+    held.append(stage(3))
+    lower(1)
     mid_copy = remote(mid_out, mid_in, m_send.at[0], m_recv.at[0], {"tp": across})
     mid_copy.start()
-    for p in (1, 2):
-        st_copies[p].wait_recv()
+    for p in range(1, PIECES - 1):
         add_piece(p)
-    up = take(parts, held_up)
     mid_copy.wait_recv()
     mid = jnp.transpose(mid_out[...] + mid_in[...]).astype(jnp.bfloat16)
-    total[:, q_cols:] += 0.5 * jnp.dot(
-        mid[:, rank:], up[:, q_cols:], preferred_element_type=jnp.float32
-    )
+    total[:, q_cols:] += 0.5 * jnp.dot(mid[:, rank:], take(2), preferred_element_type=jnp.float32)
 
     keep = pl.ds(pl.multiple_of(tp * HEAD_DIM, HEAD_DIM), HEAD_DIM)
     give = pl.ds(pl.multiple_of(across * HEAD_DIM, HEAD_DIM), HEAD_DIM)
@@ -387,7 +373,7 @@
     value_parts = []
 
     def turn(x, span):
-        return (x * cosine[span] + pltpu.roll(x, HEAD_DIM // 2, 1) * sine[span]).astype(jnp.bfloat16)
+        return (x * turns[0, span] + pltpu.roll(x, HEAD_DIM // 2, 1) * turns[1, span]).astype(jnp.bfloat16)
 
     def swap(g):
         span = pl.ds(*GROUPS[g])
@@ -435,12 +421,12 @@
 
     swap(0)
     total[:, :q_cols] += 0.5 * jnp.dot(
-        mid[:, :rank], up[:, :q_cols], preferred_element_type=jnp.float32
+        mid[:, :rank], take(3), preferred_element_type=jnp.float32
     )
     st_copies[PIECES - 1].wait_recv()
-    add_piece(PIECES - 1, slice(q_cols, None))
+    add_kv(PIECES - 1)
     swap(1)
-    add_piece(PIECES - 1, slice(0, q_cols))
+    add_q(PIECES - 1)
     attend(0)
     attend(1)
 
@@ -483,8 +469,7 @@
     cols = q_cols + kv_cols
     mine, rank = query_up_store.shape[:2]
     down_rows = jnp.transpose(down_store, (0, 2, 1))
-    parts = 3
-    lanes = half // parts
+    parts = 2
     trig = tables(tokens)
     peers = planes - 1
     vmem = pl.BlockSpec(memory_space=pltpu.VMEM)
@@ -500,20 +485,24 @@
         scratch_shapes=[
             pltpu.VMEM((tokens, half), bf16),
             pltpu.VMEM((tokens, half), bf16),
-            pltpu.VMEM((half, cols), bf16),
-            pltpu.VMEM((half, cols), bf16),
+            pltpu.VMEM((half, q_cols), bf16),
+            pltpu.VMEM((half, kv_cols), bf16),
+            pltpu.VMEM((half, q_cols), bf16),
+            pltpu.VMEM((half, kv_cols), bf16),
             pltpu.VMEM((tokens, cols), f32),
-            pltpu.VMEM((4 * mine, 2 * rank, half), bf16),
-            pltpu.VMEM((4 * mine, rank, cols), bf16),
-            pltpu.VMEM((tokens, HEAD_DIM), f32),
-            pltpu.VMEM((tokens, HEAD_DIM), f32),
+            pltpu.VMEM((parts, 4 * mine, rank, half), bf16),
+            pltpu.VMEM((4 * mine, rank, q_cols), bf16),
+            pltpu.VMEM((4 * mine, rank, kv_cols), bf16),
+            pltpu.VMEM(trig.shape, f32),
             pltpu.VMEM((16, 128), jnp.int32),
             pltpu.VMEM((peers, 16, 128), jnp.int32),
             pltpu.VMEM((planes, 4 * mine, 16, 128), bf16),
-            pltpu.VMEM((parts, peers, 2 * rank, lanes), bf16),
-            pltpu.VMEM((peers, rank, cols), bf16),
-            pltpu.VMEM((parts, peers, 2 * rank, lanes), bf16),
-            pltpu.VMEM((peers, rank, cols), bf16),
+            pltpu.VMEM((parts, peers, rank, half), bf16),
+            pltpu.VMEM((peers, rank, kv_cols), bf16),
+            pltpu.VMEM((peers, rank, q_cols), bf16),
+            pltpu.VMEM((parts, peers, rank, half), bf16),
+            pltpu.VMEM((peers, rank, kv_cols), bf16),
+            pltpu.VMEM((peers, rank, q_cols), bf16),
             pltpu.VMEM((2 * rank, tokens), f32),
             pltpu.VMEM((2 * rank, tokens), f32),
             pltpu.VMEM((tokens, kv_cols), bf16),
@@ -525,12 +514,12 @@
             dma((parts + 2,)),
             dma((parts + 2,)),
             dma((parts + 2,)),
-            dma((parts + 1,)),
-            dma((parts + 1,)),
+            dma((parts + 2,)),
+            dma((parts + 2,)),
             dma((peers,)),
             dma((peers,)),
-            dma((parts + 1, peers)),
-            dma((parts + 1, peers)),
+            dma((parts + 2, peers)),
+            dma((parts + 2, peers)),
             dma((1,)),
             dma((1,)),
             dma((len(GROUPS),)),

time: 39.4 us -> 37.3 us (0.947)
  Pallas kernels: 36.1 us -> 34.1 us
    pallas_call x1, Pallas kernels: 36.1 us -> 34.1 us  [local_fused(): pl.pallas_call(functools.partial(fused, planes), out_shape=jax.ShapeDtype...]
where the time goes in v5:
time: 37.3 us; the launch traced here: 37.2 us
  Pallas kernels  34.1 us (91%)
  local copies, waits for them, and re-layouts  1.77 us (5%)
  between operations  1.3 us (3%)
    pallas_call x1, Pallas kernels, local_fused(): pl.pallas_call(functools.partial(fused, planes), out_shape=jax.ShapeDtype...  34.1 us
    unnamed x1, local copies, waits for them, and re-layouts  1.77 us

profile of v5, /device:TPU:0, one launch (start us, length us, event | category | flops | bytes accessed | tf_op | source)
XLA Modules:
  0.0 37.2 jit_solution(3099913462242778721)
XLA Ops:
  1.3 34.1 %fused_attention.1 = bf16[256,768]{1,0:T(8,128)(2,1)} custom-call(s32[1]{0:T(128)S(6)} %copy.13.ids, s32[64]{0:T(128)} %slots.1, s32[1]{0:T(128)S(6)} %copy.12.lengths, bf16[256,1536]{1,0:T(8,128)(2,1)} %states.1, bf16[3072,768]{1,0:T(8,128)(2,1)} %wq.1, bf16[3072,256]{1,0:T(8,128)(2,1)} %wkv.1, bf16[4,32,1536]{2,1,0:T(8,128)(2,1)} %bitcast.1, ...), custom_call_target="tpu_custom_call" | custom-call | tf_op jit(solution)/shard_map/fused_attention/pallas_call | solution.py:480
  35.4 1.8 %copy.14 = bf16[256,768]{1,0:T(8,128)(2,1)} copy(bf16[256,768]{1,0:T(8,128)(2,1)} %fused_attention.1) | data formatting | bytes 786432

commit v6 on v5

--- a/solution.py
+++ b/solution.py
@@ -268,9 +268,12 @@
         )
         for k, block in enumerate(planes_of)
     ]
-    y_copies[0].start()
-    st_copies[0].start()
-    for copy in id_copies + y_copies[1:] + c_copies + st_copies[1:]:
+    def after(done, following):
+        done.wait_send()
+        for copy in following:
+            copy.start()
+
+    for copy in [y_copies[0], st_copies[0]] + id_copies + [c_copies[0]]:
         copy.start()
 
     for n in (0, 1, 2):
@@ -345,21 +348,26 @@
         )
 
     held = []
+    after(y_copies[0], [y_copies[1], c_copies[1]])
+    after(st_copies[0], [st_copies[1]])
     forward(0)
     held.append(stage(0))
+    add_piece(0)
+    after(y_copies[1], y_copies[2:] + c_copies[2:])
+    after(st_copies[1], [st_copies[2]])
     forward(1)
     held.append(stage(1))
     lower(0)
-    add_piece(0)
+    add_piece(1)
     forward(2)
     forward(3)
+    after(st_copies[2], [st_copies[3]])
     held.append(stage(2))
     held.append(stage(3))
     lower(1)
     mid_copy = remote(mid_out, mid_in, m_send.at[0], m_recv.at[0], {"tp": across})
     mid_copy.start()
-    for p in range(1, PIECES - 1):
-        add_piece(p)
+    add_piece(2)
     mid_copy.wait_recv()
     mid = jnp.transpose(mid_out[...] + mid_in[...]).astype(jnp.bfloat16)
     total[:, q_cols:] += 0.5 * jnp.dot(mid[:, rank:], take(2), preferred_element_type=jnp.float32)
@@ -430,7 +438,7 @@
     attend(0)
     attend(1)
 
-    for copy in id_copies + st_copies + y_copies + c_copies + f_copies + [mid_copy] + kv_copies:
+    for copy in id_copies + st_copies[3:] + y_copies[2:] + c_copies + f_copies + [mid_copy] + kv_copies:
         copy.wait_send()
     for sent in z_copies:
         for copy in sent:

time: 37.3 us -> 37.5 us (level)
  no operation moved by 1% of the time
where the time goes in v6:
time: 37.5 us; the launch traced here: 37.3 us
  Pallas kernels  34.2 us (91%)
  local copies, waits for them, and re-layouts  1.77 us (5%)
  between operations  1.3 us (3%)
    pallas_call x1, Pallas kernels, local_fused(): pl.pallas_call(functools.partial(fused, planes), out_shape=jax.ShapeDtype...  34.2 us
    unnamed x1, local copies, waits for them, and re-layouts  1.77 us

profile of v6, /device:TPU:0, one launch (start us, length us, event | category | flops | bytes accessed | tf_op | source)
XLA Modules:
  0.0 37.3 jit_solution(17043804496137290264)
XLA Ops:
  1.3 34.2 %fused_attention.1 = bf16[256,768]{1,0:T(8,128)(2,1)} custom-call(s32[1]{0:T(128)S(6)} %copy.13.ids, s32[64]{0:T(128)} %slots.1, s32[1]{0:T(128)S(6)} %copy.12.lengths, bf16[256,1536]{1,0:T(8,128)(2,1)} %states.1, bf16[3072,768]{1,0:T(8,128)(2,1)} %wq.1, bf16[3072,256]{1,0:T(8,128)(2,1)} %wkv.1, bf16[4,32,1536]{2,1,0:T(8,128)(2,1)} %bitcast.1, ...), custom_call_target="tpu_custom_call" | custom-call | tf_op jit(solution)/shard_map/fused_attention/pallas_call | solution.py:488
  35.5 1.8 %copy.14 = bf16[256,768]{1,0:T(8,128)(2,1)} copy(bf16[256,768]{1,0:T(8,128)(2,1)} %fused_attention.1) | data formatting | bytes 786432

commit v7 on v6

--- a/solution.py
+++ b/solution.py
@@ -120,6 +120,7 @@
 
 MESH = pl.DeviceIdType.MESH
 PIECES = 4
+SENDS = 8
 GROUPS = ((0, 192), (192, 64))
 
 
@@ -186,6 +187,7 @@
     q_cols = wq.shape[1]
     tokens = own_st.shape[0]
     step = tokens // PIECES
+    slab = tokens // SENDS
     parts = plane_down.shape[0]
     mine, rank = plane_q.shape[0] // per_plane, plane_q.shape[1]
     core_peer = r + 1 - 2 * (r % 2)
@@ -228,6 +230,8 @@
     for peer in [core_peer, y_peer] + z_peers:
         pl.semaphore_signal(barrier, inc=1, device_id={"req": peer}, device_id_type=MESH)
     pl.semaphore_signal(barrier, inc=1, device_id={"tp": across}, device_id_type=MESH)
+    for n in (0, 6, 7, 8, 9):
+        loads[n].wait()
     pl.semaphore_wait(barrier, planes + 2)
 
     id_copies = [
@@ -236,21 +240,21 @@
     ]
     st_copies = [
         remote(
-            states.at[pl.ds(p * step, step)],
-            other_st.at[pl.ds(p * step, step)],
+            own_st.at[pl.ds(p * slab, slab)],
+            other_st.at[pl.ds(p * slab, slab)],
             st_send.at[p],
             st_recv.at[p],
             {"tp": across},
         )
-        for p in range(PIECES)
+        for p in range(SENDS)
     ]
     def share(peer, send, recv):
         ends = [
-            (down_rows.at[:, pl.ds(k * rank, rank)], plane_down.at[k, place(r)]) for k in range(parts)
-        ] + [(pair_rows, plane_kv.at[place(r)]), (query_rows, plane_q.at[place(r)])]
+            plane_down.at[k, place(r)] for k in range(parts)
+        ] + [plane_kv.at[place(r)], plane_q.at[place(r)]]
         return [
-            remote(source, target, send.at[n], recv.at[n], {"req": peer})
-            for n, (source, target) in enumerate(ends)
+            remote(block, block, send.at[n], recv.at[n], {"req": peer})
+            for n, block in enumerate(ends)
         ]
 
     planes_of = [plane_down.at[k] for k in range(parts)] + [plane_kv, plane_q]
@@ -273,15 +277,15 @@
         for copy in following:
             copy.start()
 
-    for copy in [y_copies[0], st_copies[0]] + id_copies + [c_copies[0]]:
+    for copy in [y_copies[0], st_copies[0]] + id_copies + [c_copies[0]] + st_copies[1:3]:
         copy.start()
 
-    for n in (0, 1, 2):
+    for n in (1, 2):
         loads[n].wait()
     total[:, :q_cols] = jnp.dot(own_st[...], wq_own[...], preferred_element_type=jnp.float32)
     total[:, q_cols:] = jnp.dot(own_st[...], wkv_own[...], preferred_element_type=jnp.float32)
-    for copy in loads[3:]:
-        copy.wait()
+    for n in (3, 4, 5):
+        loads[n].wait()
     for copy in id_copies:
         copy.wait_recv()
 
@@ -297,8 +301,12 @@
             other_st[span], wkv_other[...], preferred_element_type=jnp.float32
         )
 
+    def arrived(p):
+        for n in range(p * SENDS // PIECES, (p + 1) * SENDS // PIECES):
+            st_copies[n].wait_recv()
+
     def add_piece(p):
-        st_copies[p].wait_recv()
+        arrived(p)
         add_kv(p)
         add_q(p)
 
@@ -348,20 +356,22 @@
         )
 
     held = []
+    after(st_copies[0], [st_copies[3]])
     after(y_copies[0], [y_copies[1], c_copies[1]])
-    after(st_copies[0], [st_copies[1]])
     forward(0)
+    after(st_copies[1], [st_copies[4]])
     held.append(stage(0))
     add_piece(0)
+    after(st_copies[2], [st_copies[5]])
     after(y_copies[1], y_copies[2:] + c_copies[2:])
-    after(st_copies[1], [st_copies[2]])
     forward(1)
+    after(st_copies[3], [st_copies[6]])
     held.append(stage(1))
     lower(0)
     add_piece(1)
+    after(st_copies[4], [st_copies[7]])
     forward(2)
     forward(3)
-    after(st_copies[2], [st_copies[3]])
     held.append(stage(2))
     held.append(stage(3))
     lower(1)
@@ -431,14 +441,14 @@
     total[:, :q_cols] += 0.5 * jnp.dot(
         mid[:, :rank], take(3), preferred_element_type=jnp.float32
     )
-    st_copies[PIECES - 1].wait_recv()
+    arrived(PIECES - 1)
     add_kv(PIECES - 1)
     swap(1)
     add_q(PIECES - 1)
     attend(0)
     attend(1)
 
-    for copy in id_copies + st_copies[3:] + y_copies[2:] + c_copies + f_copies + [mid_copy] + kv_copies:
+    for copy in id_copies + st_copies[5:] + y_copies[2:] + c_copies + f_copies + [mid_copy] + kv_copies:
         copy.wait_send()
     for sent in z_copies:
         for copy in sent:
@@ -516,8 +526,8 @@
             pltpu.VMEM((tokens, kv_cols), bf16),
             pltpu.VMEM((tokens, HEAD_DIM), bf16),
             dma((10,)),
-            dma((PIECES,)),
-            dma((PIECES,)),
+            dma((SENDS,)),
+            dma((SENDS,)),
             dma((parts + 2,)),
             dma((parts + 2,)),
             dma((parts + 2,)),

time: 37.5 us -> 37.7 us (level)
  no operation moved by 1% of the time
where the time goes in v7:
time: 37.7 us; the launch traced here: 37.5 us
  Pallas kernels  34.4 us (91%)
  local copies, waits for them, and re-layouts  1.77 us (5%)
  between operations  1.3 us (3%)
    pallas_call x1, Pallas kernels, local_fused(): pl.pallas_call(functools.partial(fused, planes), out_shape=jax.ShapeDtype...  34.4 us
    unnamed x1, local copies, waits for them, and re-layouts  1.77 us

profile of v7, /device:TPU:0, one launch (start us, length us, event | category | flops | bytes accessed | tf_op | source)
XLA Modules:
  0.0 37.5 jit_solution(6296314486415868140)
XLA Ops:
  1.3 34.4 %fused_attention.1 = bf16[256,768]{1,0:T(8,128)(2,1)} custom-call(s32[1]{0:T(128)S(6)} %copy.13.ids, s32[64]{0:T(128)} %slots.1, s32[1]{0:T(128)S(6)} %copy.12.lengths, bf16[256,1536]{1,0:T(8,128)(2,1)} %states.1, bf16[3072,768]{1,0:T(8,128)(2,1)} %wq.1, bf16[3072,256]{1,0:T(8,128)(2,1)} %wkv.1, bf16[4,32,1536]{2,1,0:T(8,128)(2,1)} %bitcast.1, ...), custom_call_target="tpu_custom_call" | custom-call | tf_op jit(solution)/shard_map/fused_attention/pallas_call | solution.py:498
  35.7 1.8 %copy.14 = bf16[256,768]{1,0:T(8,128)(2,1)} copy(bf16[256,768]{1,0:T(8,128)(2,1)} %fused_attention.1) | data formatting | bytes 786432
